TPU v7x, 256 devices: a whole 4x4x8 slice. The times are simulated.
256 devices in a mesh: segment: 4 (over y), seq: 32 (over z, x_lo, core), tensor: 2 (over x_hi).
Axes of the slice: x: 4 (x_hi: 2, x_lo: 2; x = x_hi * 2 + x_lo), y: 4, z: 8, core: 2. Of those that a mesh axis runs over, the one named last changes fastest.
Arguments:
- self_q: bfloat16 [4, 4096, 32, 128], P('segment', 'seq', 'tensor'), may hold values from -24 to 24
- self_kv: bfloat16 [4, 4096, 4, 256], P('segment', 'seq', 'tensor'), may hold values from -4.5 to 4.5
- cross_q: bfloat16 [4, 4096, 32, 128], P('segment', 'seq', 'tensor'), may hold values from -24 to 24
- vision_kv: bfloat16 [1024, 4, 256], P(('segment', 'seq'), 'tensor'), may hold values from -4.5 to 4.5
- cross_gate: float32 [4, 32], P('segment', 'tensor'), may hold values from 0.3 to 1.5
- cross_mask: int32 [64, 4], P('seq'), may hold values 0 or 1
- image_tokens: int32 [4], replicated, may hold values from 1 to 512, 1024 in all
- out_cotangent: bfloat16 [4, 4096, 32, 128], P('segment', 'seq', 'tensor'), may hold values from -6 to 6
Outputs:
- mixed: bfloat16 [4, 4096, 32, 128], P('segment', 'seq', 'tensor')
- grad_cross_q: bfloat16 [4, 4096, 32, 128], P('segment', 'seq', 'tensor')
- grad_vision_kv: float32 [1024, 4, 256], P(('segment', 'seq'), 'tensor')
Inputs may be any that keep to these rules, and one draw needn't show every extreme that they name: `image_tokens`: the counts sum to 1024.
All inputs are finite; a program needn't handle non-finite values. No bound on the sum of `cross_mask` on one device may be relied on, other than what follows from the above.
Results may differ from a plain program's by a relative error of at most 0.02.
Values may be sent and summed in bfloat16 or wider, within the bound.
No kernel may reach another device: no remote copies, remote signals or barrier semaphores. Data moves between devices by JAX's collectives and lax.ppermute only.
A program may use at most 64 MiB of HBM per device.

v0:
```python
import math

import jax
import jax.numpy as jnp
from jax import lax
from jax.sharding import PartitionSpec as P

IMAGES = 4
BLOCK = 64


def image_index(image_tokens, token_count):
    bounds = jnp.cumsum(image_tokens)
    column = jnp.arange(token_count, dtype=jnp.int32)
    return jnp.sum((column[:, None] >= bounds[None, :-1]).astype(jnp.int32), axis=1)


def shards(
    self_q, self_kv, cross_q, vision_kv, cross_gate, cross_mask, image_tokens, out_cotangent
):
    row_count = self_q.shape[1]
    head_count = self_q.shape[2]
    head_width = self_q.shape[3]
    kv_count = self_kv.shape[2]
    groups = head_count // kv_count
    score_scale = 1.0 / math.sqrt(head_width)
    first_row = lax.axis_index("seq") * row_count
    row_ids = first_row + jnp.arange(row_count, dtype=jnp.int32)
    last_row = first_row + row_count - 1
    queries = self_q[0].reshape(row_count, kv_count, groups, head_width)

    def update_state(state_in, key_piece, offset):
        run_max, run_sum, run_acc = state_in
        scores = (
            jnp.einsum(
                "rkgd,nkd->kgrn",
                queries,
                key_piece[:, :, :head_width],
                preferred_element_type=jnp.float32,
            )
            * score_scale
        )
        columns = offset + jnp.arange(key_piece.shape[0], dtype=jnp.int32)
        causal = columns[None, :] <= row_ids[:, None]
        new_max = jnp.maximum(run_max, jnp.max(jnp.where(causal, scores, -1e30), axis=-1))
        factor = jnp.exp(run_max - new_max)
        weights = jnp.where(causal, jnp.exp(scores - new_max[..., None]), 0.0)
        run_sum = run_sum * factor + jnp.sum(weights, axis=-1)
        run_acc = run_acc * factor[..., None] + jnp.einsum(
            "kgrn,nkd->kgrd",
            weights.astype(jnp.bfloat16),
            key_piece[:, :, head_width:],
            preferred_element_type=jnp.float32,
        )
        return (new_max, run_sum, run_acc)

    def key_block(state_in, inputs):
        key_piece, offset = inputs
        state_out = lax.cond(
            offset > last_row,
            lambda unchanged: unchanged,
            lambda current: update_state(current, key_piece, offset),
            state_in,
        )
        return (state_out, None)

    start_state = (
        jnp.full((kv_count, groups, row_count), -1e30, jnp.float32),
        jnp.zeros((kv_count, groups, row_count), jnp.float32),
        jnp.zeros((kv_count, groups, row_count, head_width), jnp.float32),
    )
    shard_piece = lax.all_gather(self_kv, "seq", axis=1, tiled=True)
    piece_rows = shard_piece.shape[1]
    stride = math.gcd(piece_rows, 512)
    pieces = shard_piece[0].reshape(piece_rows // stride, stride, kv_count, 2 * head_width)
    offsets = stride * jnp.arange(piece_rows // stride, dtype=jnp.int32)
    state_out, unused = lax.scan(key_block, start_state, (pieces, offsets))
    run_max, run_sum, run_acc = state_out
    self_out = run_acc / run_sum[..., None]
    images = lax.all_gather(vision_kv, ("segment", "seq"), axis=0, tiled=True)
    vision_keys = images[:, :, :head_width]
    vision_values = images[:, :, head_width:]
    image_of = image_index(image_tokens, images.shape[0])
    one_hot = (image_of[None, :] == jnp.arange(IMAGES, dtype=jnp.int32)[:, None]).astype(
        jnp.float32
    )
    text_mask = jnp.repeat(cross_mask, BLOCK, axis=0).astype(jnp.float32)
    live_rows = jnp.dot(text_mask, one_hot, precision=lax.Precision.HIGHEST) > 0.5
    cross_rows = cross_q[0].reshape(row_count, kv_count, groups, head_width)
    cross_scores = (
        jnp.einsum("rkgd,nkd->kgrn", cross_rows, vision_keys, preferred_element_type=jnp.float32)
        * score_scale
    )
    cross_max = jnp.max(jnp.where(live_rows, cross_scores, -1e30), axis=-1)
    cross_weights = jnp.where(live_rows, jnp.exp(cross_scores - cross_max[..., None]), 0.0)
    cross_total = jnp.maximum(jnp.sum(cross_weights, axis=-1), 1.0)
    cross_out = (
        jnp.einsum(
            "kgrn,nkd->kgrd",
            cross_weights.astype(jnp.bfloat16),
            vision_values,
            preferred_element_type=jnp.float32,
        )
        / cross_total[..., None]
    )
    gate_value = jnp.tanh(cross_gate[0]).reshape(kv_count, groups)
    mixed_rows = self_out + gate_value[:, :, None, None] * cross_out
    mixed_rows = (
        jnp.transpose(mixed_rows, (2, 0, 1, 3))
        .reshape(1, row_count, head_count, head_width)
        .astype(jnp.bfloat16)
    )
    cotangent_rows = out_cotangent[0].reshape(row_count, kv_count, groups, head_width)
    grad_out = (gate_value[None, :, :, None] * cotangent_rows.astype(jnp.float32)).astype(
        jnp.bfloat16
    )
    row_dot = jnp.sum(
        jnp.transpose(grad_out, (1, 2, 0, 3)).astype(jnp.float32) * cross_out, axis=-1
    )
    cross_probs = cross_weights / cross_total[..., None]
    prob_grad = jnp.einsum(
        "rkgd,nkd->kgrn", grad_out, vision_values, preferred_element_type=jnp.float32
    )
    score_grad = (cross_probs * (prob_grad - row_dot[..., None]) * score_scale).astype(jnp.bfloat16)
    query_grad = jnp.einsum(
        "kgrn,nkd->rkgd", score_grad, vision_keys, preferred_element_type=jnp.float32
    )
    query_grad = query_grad.reshape(1, row_count, head_count, head_width).astype(jnp.bfloat16)
    key_part = jnp.einsum(
        "kgrn,rkgd->nkd", score_grad, cross_rows, preferred_element_type=jnp.float32
    )
    value_part = jnp.einsum(
        "kgrn,rkgd->nkd",
        cross_probs.astype(jnp.bfloat16),
        grad_out,
        preferred_element_type=jnp.float32,
    )
    partial_grads = jnp.concatenate([key_part, value_part], axis=-1)
    image_grads = lax.psum_scatter(
        partial_grads, ("segment", "seq"), scatter_dimension=0, tiled=True
    )
    return (mixed_rows, query_grad, image_grads)


def solution(mesh):
    placed = (
        P("segment", "seq", "tensor", None),
        P("segment", "seq", "tensor", None),
        P("segment", "seq", "tensor", None),
        P(("segment", "seq"), "tensor", None),
        P("segment", "tensor"),
        P("seq", None),
        P(),
        P("segment", "seq", "tensor", None),
    )
    return jax.shard_map(
        shards,
        mesh=mesh,
        in_specs=placed,
        out_specs=(
            P("segment", "seq", "tensor", None),
            P("segment", "seq", "tensor", None),
            P(("segment", "seq"), "tensor", None),
        ),
        check_vma=False,
    )
```

profile of v0, /device:TPU:4, one launch (start us, length us, event | category | flops | bytes accessed | tf_op | source)
XLA Modules:
  0.0 1447.9 jit_solution(3719315225802829949)
XLA Ops:
  7.2 0.0 all-gather.5.cloned.1.call-start
  7.2 1.3 copy.71
  8.5 0.0 all-gather.5.cloned.1.call-update
  8.5 0.0 all-gather.3.cloned.1.call-start
  8.6 1.6 copy.67
  10.2 0.0 all-gather.3.cloned.1.call-update
  10.2 0.0 all-reduce.3.cloned.1.call-start
  10.2 1.5 copy.75
  11.7 0.7 tanh_reduce_fusion
  12.4 0.1 tanh.15
  12.5 1.2 copy.68
  13.6 0.7 convert_element_type.77
  14.3 0.8 reduce-window.4
  15.1 1.5 copy.80
  16.6 0.0 copy-start.2
  16.6 0.1 convert_reduce_fusion
  16.7 0.5 fusion.40
  17.2 194.8 %all-gather.5.cloned.1.call-done = bf16[1024,2,256]{2,0,1:T(8,128)(2,1)} async-done(((bf16[8,2,256]{2,0,1:T(8,128)(2,1)}), bf16[1024,2,256]{2,0,1:T(8,128)(2,1)}) %all-gather.5.cloned.1.call-update) | async-done | bytes 1048592 | tf_op jit(solution)/shard_map/all_gather | solution.py:80
  212.1 7.6 fusion.50
  219.7 0.0 copy-done.2
  219.7 59.5 %all-gather.3.cloned.1.call-done = bf16[1,4096,2,256]{3,1,2,0:T(8,128)(2,1)} async-done(((bf16[1,128,2,256]{3,1,2,0:T(8,128)(2,1)}), bf16[1,4096,2,256]{3,1,2,0:T(8,128)(2,1)}) %all-gather.3.cloned.1.call-update) | async-done | bytes 4194320 | tf_op jit(solution)/shard_map/all_gather | solution.py:72
  279.2 4.5 copy.69
  283.7 0.1 broadcast_in_dim.54
  283.8 15.8 %while.15 = (s32[]{:T(128)}, f32[2,8,128]{2,1,0:T(8,128)S(1)}, f32[2,8,128]{2,1,0:T(8,128)S(1)}, f32[2,8,128,128]{3,2,1,0:T(8,128)S(1)}, s32[8]{0:T(128)S(1)}, /...) while((s32[]{:T(128)}, f32[2,8,128]{2,1,0:T(8,128)S(1)}, ...), condition=%wide.region_5.6_spmd.clone, body=%wide.region_0.5_spmd.clone.sunk | while | flops 548999808 | bytes 17176844 | solution.py:77
  284.0 0.6 dynamic_slice.13
  285.3 5.1 conditional.3
  285.3 0.7 iota_add_fusion
  286.0 0.1 broadcast_compare_fusion
  286.1 1.1 dynamic-slice_bitcast_fusion
  287.2 0.8 fusion.2
  288.0 0.8 fusion.6
  288.8 1.5 fusion.13
  290.4 0.6 dynamic_slice.13
  291.7 0.6 dynamic_slice.13
  293.0 0.6 dynamic_slice.13
  294.4 0.6 dynamic_slice.13
  295.7 0.6 dynamic_slice.13
  297.0 0.6 dynamic_slice.13
  298.3 0.6 dynamic_slice.13
  299.6 0.3 copy.70
  300.0 0.0 copy-start.1
  300.0 4.6 fusion.41
  304.6 1.3 copy-done.1
  305.9 0.0 copy-start.4
  305.9 1.5 fusion.34
  307.4 0.0 copy-done.4
  307.4 0.0 copy-start.3
  307.4 1.8 fusion.22
  309.2 0.0 copy-start
  309.3 1.9 copy-done
  311.2 0.0 copy-done.3
  311.2 1.5 convolution_bitcast_fusion
  312.6 0.1 pad_maximum_fusion
  312.8 0.0 copy-start.5
  312.8 2.4 copy.82
  315.2 0.0 all-reduce.3.cloned.1.call-update
  315.2 0.0 copy-done.5
  315.2 0.6 dynamic-slice
  316.5 1.2 copy.83
  317.7 4.0 convolution_convert_fusion
  321.7 1.1 copy.84
  322.8 1117.2 %all-reduce.3.cloned.1.call-done = f32[1024,2,256]{2,1,0:T(2,128)} async-done(((f32[1024,2,256]{2,1,0:T(2,128)}), f32[1024,2,256]{2,1,0:T(2,128)}) %all-reduce.3.cloned.1.call-update) | async-done | bytes 2097168
  1440.0 1.3 constant_dynamic-slice_fusion
  (39 shorter events, 0.3 us)
Async XLA Ops:
  7.2 204.9 %all-gather.5.cloned.1.call-start = ((), (), s32[]{:S(2)}) async-start(), calls=%async_computation.1 | async-start | bytes 1056768 | tf_op jit(solution)/shard_map/all_gather | solution.py:80
  8.5 270.7 %all-gather.3.cloned.1.call-start = ((), (), s32[]{:S(2)}) async-start(), calls=%async_computation | async-start | bytes 4325376 | tf_op jit(solution)/shard_map/all_gather | solution.py:72
  10.2 1429.8 %all-reduce.3.cloned.1.call-start = ((), (), s32[]{:S(2)}) async-start(), calls=%async_computation.2 | async-start | bytes 4194304
  16.6 203.1 %copy-start.2 = (bf16[128,2,8,128]{0,3,2,1:T(8,128)(2,1)}, bf16[128,2,8,128]{0,3,2,1:T(8,128)(2,1)S(1)}, u32[]{:S(2)}) copy-start(bf16[128,2,8,128]{0,3,2,1:T(8,128)(2,1)S(1)} %copy.80) | copy-start | bytes 1572868
  300.0 5.9 copy-start.1
  305.9 1.5 copy-start.4
  307.4 3.8 copy-start.3
  309.2 1.9 copy-start
  312.8 2.4 copy-start.5
Sparse Core Ops, SparseCore 0:
  10.4 201.6 all-gather.4
  214.5 64.6 all-gather.2
  315.3 1124.6 all-reduce.2
where the time goes:
time: 1450 us
  waiting for transfers between devices  1370 us (94%)
  local copies, waits for them, and re-layouts  28.3 us (2%)
  matrix products  23.8 us (2%)
  between operations  14.6 us (1%)
    unnamed x4, waiting for transfers between devices  1120 us
    all_gather x1, waiting for transfers between devices, shards(): images = lax.all_gather(vision_kv, ('segment', 'seq'), axis=0, tiled=True)  195 us
    all_gather x1, waiting for transfers between devices, shards(): shard_piece = lax.all_gather(self_kv, 'seq', axis=1, tiled=True)  59.5 us
  transfers between devices with their start and end apart: 3, of which 3 were waited for; matrix products, arithmetic and copies ran while one was open for 2% of the time, Pallas kernels for 0%

commit v1 on v0

v1 whole, which is shorter than its diff:
```python
import math

import jax
import jax.numpy as jnp
from jax import lax
from jax.experimental import pallas as pl
from jax.experimental.pallas import tpu as pltpu
from jax.sharding import Mesh, PartitionSpec as P

IMAGES = 4
BLOCK = 64
HD = 128
NEG = -1e30
F32 = jnp.float32
BF16 = jnp.bfloat16
SCALE = 1.0 / math.sqrt(HD)
SCALE2 = SCALE / math.log(2.0)
NT = (((1,), (1,)), ((), ()))


def nt(a, b):
    return lax.dot_general(a, b, NT, preferred_element_type=F32)


def nn(a, b):
    return jnp.dot(a, b, preferred_element_type=F32)


def flip(a):
    return jnp.transpose(a.astype(F32), (1, 0)).astype(a.dtype)


def cross_kernel(
    info_ref,
    cq_ref,
    cot_ref,
    gate_col_ref,
    gate_row_ref,
    va_ref,
    vb_ref,
    out_ref,
    gq_ref,
    ga_ref,
    gb_ref,
    bias_ref,
):
    half = va_ref.shape[0]
    core = info_ref[11]
    pos = lax.broadcasted_iota(jnp.int32, (half, HD), 0)
    for side in range(2):
        which = core if side == 0 else 1 - core
        token = (2 * (pos // 8) + which) * 8 + pos % 8
        for rb in range(2):
            on = jnp.zeros((half, HD), jnp.int32) + info_ref[3 + rb * IMAGES]
            for k in range(IMAGES - 1):
                on = jnp.where(token >= info_ref[k], info_ref[3 + rb * IMAGES + k + 1], on)
            bias_ref[rb, pl.ds(side * half, half), :] = jnp.where(on == 1, 0.0, NEG)

    rows = BLOCK * 8
    for h in range(2):
        lane = h * 2 * HD
        ka, kb = va_ref[:, lane : lane + HD], vb_ref[:, lane : lane + HD]
        wa, wb = va_ref[:, lane + HD : lane + 2 * HD], vb_ref[:, lane + HD : lane + 2 * HD]
        keys = jnp.concatenate([ka, kb], axis=0)
        values = jnp.concatenate([wa, wb], axis=0)
        keys_t, values_t = flip(keys), flip(values)
        gk = None
        for rb in range(2):
            r0 = rb * BLOCK
            q = cq_ref[r0 : r0 + BLOCK, h * 8 : h * 8 + 8, :].reshape(rows, HD)
            cot = cot_ref[r0 : r0 + BLOCK, h * 8 : h * 8 + 8, :].astype(F32)
            go = (cot * gate_col_ref[h * 8 : h * 8 + 8, :][None]).astype(BF16).reshape(rows, HD)
            s = nt(keys, q) * SCALE2 + jnp.tile(bias_ref[rb], (1, rows // HD))
            top = jnp.max(s, axis=0, keepdims=True)
            top = jnp.where(top < 0.5 * NEG, 0.0, top)
            p = jnp.exp2(s - top)
            inv = 1.0 / jnp.maximum(jnp.sum(p, axis=0, keepdims=True), 1.0)
            pb = p.astype(BF16)
            cross = nn(values_t, pb) * inv
            out_ref[h, :, rb * rows : (rb + 1) * rows] = cross * gate_row_ref[h : h + 1, :]
            go_t = jnp.transpose(go.astype(F32), (1, 0))
            dot = jnp.sum(go_t * cross, axis=0, keepdims=True)
            ds = (p * (nt(values, go) - dot)).astype(BF16)
            dq = nn(keys_t, ds) * (inv * SCALE)
            gq_ref[r0 : r0 + BLOCK, h * 8 : h * 8 + 8, :] = (
                jnp.transpose(dq, (1, 0)).reshape(BLOCK, 8, HD).astype(BF16)
            )
            inv_col = jnp.transpose(jnp.broadcast_to(inv, (HD, rows)), (1, 0))
            qs = (q.astype(F32) * (inv_col * SCALE)).astype(BF16)
            gs = (go.astype(F32) * inv_col).astype(BF16)
            dk, dv = nn(ds, qs), nn(pb, gs)
            if rb == 0:
                gk, gv = dk, dv
            else:
                gk, gv = gk + dk, gv + dv
        ga_ref[:, lane : lane + HD] = gk[:half]
        ga_ref[:, lane + HD : lane + 2 * HD] = gv[:half]
        gb_ref[:, lane : lane + HD] = gk[half:].astype(BF16)
        gb_ref[:, lane + HD : lane + 2 * HD] = gv[half:].astype(BF16)


CHUNK = 512


def self_kernel(info_ref, q_ref, kva_ref, kvb_ref, cross_ref, out_ref, acc_ref, top_ref, sum_ref):
    own = info_ref[0]
    core = info_ref[1]
    rows = BLOCK * 8
    acc_ref[...] = jnp.zeros_like(acc_ref)
    top_ref[...] = jnp.full_like(top_ref, NEG)
    sum_ref[...] = jnp.zeros_like(sum_ref)

    def step(kv_ref, chunk, limits):
        start = pl.multiple_of(chunk * CHUNK, CHUNK)
        for h in range(2):
            lane = h * 2 * HD
            keys = kv_ref[pl.ds(start, CHUNK), lane : lane + HD]
            values_t = flip(kv_ref[pl.ds(start, CHUNK), lane + HD : lane + 2 * HD])
            for rb in range(2):
                r0 = rb * BLOCK
                cols = slice(rb * rows, (rb + 1) * rows)
                q = q_ref[r0 : r0 + BLOCK, h * 8 : h * 8 + 8, :].reshape(rows, HD)
                s = nt(keys, q) * SCALE2
                if limits is not None:
                    key = lax.broadcasted_iota(jnp.int32, (CHUNK, rows), 0)
                    s = jnp.where(key <= limits[rb] - start, s, NEG)
                old = top_ref[h : h + 1, cols]
                top = jnp.maximum(old, jnp.max(s, axis=0, keepdims=True))
                factor = jnp.exp2(old - top)
                p = jnp.exp2(s - top)
                sum_ref[h : h + 1, cols] = sum_ref[h : h + 1, cols] * factor + jnp.sum(
                    p, axis=0, keepdims=True
                )
                top_ref[h : h + 1, cols] = top
                acc_ref[h, :, cols] = acc_ref[h, :, cols] * factor + nn(values_t, p.astype(BF16))

    def side(kv_ref, full, limits, partial):
        @pl.loop(0, full)
        def _(chunk):
            step(kv_ref, chunk, None)

        @pl.when(partial)
        def _():
            step(kv_ref, full, limits)

    row = lax.broadcasted_iota(jnp.int32, (1, rows), 1) // 8
    per = CHUNK // 128
    side(kva_ref, own // per, [own * 128 + rb * BLOCK + row for rb in range(2)], own >= 0)
    count = own + core
    side(kvb_ref, count // per, [0 * row + count * 128 - 1] * 2, count % per > 0)
    for h in range(2):
        mixed = acc_ref[h] * (1.0 / sum_ref[h : h + 1, :]) + cross_ref[h]
        out_ref[:, h * 8 : h * 8 + 8, :] = (
            jnp.transpose(mixed, (1, 0)).reshape(2 * BLOCK, 8, HD).astype(BF16)
        )


def spec():
    return pl.BlockSpec(memory_space=pltpu.VMEM)


def shards(
    self_q, self_kv, cross_q, vision_kv, cross_gate, cross_mask, image_tokens, out_cotangent
):
    x = lax.axis_index("x")
    core = lax.axis_index("c")
    swap = [(0, 1), (1, 0)]
    ring = ("y", "z", "x")
    parts = lax.axis_size(ring)
    kv = self_kv.reshape(128, 4 * HD)
    other = lax.ppermute(kv, "x", swap)
    pair = jnp.where(x == 0, jnp.stack([kv, other]), jnp.stack([other, kv]))
    kva = lax.all_gather(pair.reshape(256, 4 * HD), "z", axis=0, tiled=True)
    kvb = lax.ppermute(kva, "c", swap)

    image = vision_kv.reshape(8, 4 * HD)
    tokens = parts * 8
    va = lax.all_to_all(
        jnp.broadcast_to(image[None], (parts, 8, 4 * HD)), ring, 0, 0, tiled=True
    ).reshape(tokens, 4 * HD)
    vb = lax.ppermute(va, "c", swap)

    gate = jnp.tanh(cross_gate[0])
    gate_col = jnp.broadcast_to(gate[:, None], (16, HD))
    gate_row = jnp.tile(gate.reshape(2, 8), (1, BLOCK))
    bounds = jnp.cumsum(image_tokens)[: IMAGES - 1]
    info = jnp.concatenate(
        [bounds, cross_mask.reshape(2 * IMAGES), jnp.stack([core, core])]
    ).astype(jnp.int32)

    smem = pl.BlockSpec(memory_space=pltpu.SMEM)
    cross_t, grad_q, grad_own, grad_other = pl.pallas_call(
        cross_kernel,
        out_shape=(
            jax.ShapeDtypeStruct((2, HD, 1024), F32),
            jax.ShapeDtypeStruct((128, 16, HD), BF16),
            jax.ShapeDtypeStruct((tokens, 4 * HD), F32),
            jax.ShapeDtypeStruct((tokens, 4 * HD), BF16),
        ),
        in_specs=[smem] + [spec()] * 6,
        out_specs=[spec()] * 4,
        scratch_shapes=[pltpu.VMEM((2, 2 * tokens, HD), F32)],
        compiler_params=pltpu.CompilerParams(vmem_limit_bytes=48 << 20),
        cost_estimate=pl.CostEstimate(
            flops=6 * 2 * 2 * 1024 * 1024 * 128, bytes_accessed=6 << 20, transcendentals=2 << 20
        ),
        name="cross_attention",
    )(info, cross_q[0], out_cotangent[0], gate_col, gate_row, va, vb)

    received = lax.ppermute(grad_other, "c", swap)
    partial = (grad_own + received.astype(F32)).astype(BF16).reshape(parts, 8, 4 * HD)
    pieces = lax.all_to_all(partial, ring, 0, 0, tiled=True)

    own = lax.axis_index("z") * 2 + x
    mixed = pl.pallas_call(
        self_kernel,
        out_shape=jax.ShapeDtypeStruct((128, 16, HD), BF16),
        in_specs=[smem] + [spec()] * 4,
        out_specs=spec(),
        scratch_shapes=[
            pltpu.VMEM((2, HD, 1024), F32),
            pltpu.VMEM((2, 1024), F32),
            pltpu.VMEM((2, 1024), F32),
        ],
        compiler_params=pltpu.CompilerParams(vmem_limit_bytes=48 << 20),
        cost_estimate=pl.CostEstimate(
            flops=2 * 2 * 2 * 4096 * 1024 * 128, bytes_accessed=6 << 20, transcendentals=8 << 20
        ),
        name="self_attention",
    )(jnp.stack([own, core]).astype(jnp.int32), self_q[0], kva, kvb, cross_t)

    image_grads = jnp.sum(pieces.astype(F32), axis=0).reshape(8, 2, 2 * HD)
    return (mixed[None], grad_q[None], image_grads)


def solution(mesh):
    fine = Mesh(mesh.devices.reshape(4, 8, 2, 2, 2), ("y", "z", "x", "c", "t"))
    rows = P("y", ("z", "x", "c"), "t", None)
    image = P(("y", "z", "x", "c"), "t", None)
    return jax.shard_map(
        shards,
        mesh=fine,
        in_specs=(rows, rows, rows, image, P("y", "t"), P(("z", "x", "c"), None), P(), rows),
        out_specs=(rows, rows, image),
        check_vma=False,
    )
```

time: 1450 us -> 132 us (0.09)
  the two profiles are of different devices: /device:TPU:4 before, /device:TPU:193 now
where the time goes in v1:
time: 132 us; the launch traced here: 131 us
  waiting for transfers between devices  31.2 us (24%)
  Pallas kernels  30.4 us (23%)
  blocking collectives  27.9 us (21%)
  starting transfers between devices  19.6 us (15%)
  between operations  14.1 us (11%)
  local copies, waits for them, and re-layouts  5.94 us (4%)
  other arithmetic  2.12 us (2%)
    all_to_all x1, blocking collectives, shards(): lax.all_to_all(jnp.broadcast_to(image[None], (parts, 8, 4 * HD)), ring, 0...  27.9 us
    pallas_call x1, Pallas kernels, shards(): pl.pallas_call(self_kernel, out_shape=jax.ShapeDtypeStruct((128, 16, HD),...  21.2 us
    all_to_all x1, waiting for transfers between devices, shards(): pieces = lax.all_to_all(partial, ring, 0, 0, tiled=True)  16 us
    all_gather x1, waiting for transfers between devices, shards(): kva = lax.all_gather(pair.reshape(256, 4 * HD), 'z', axis=0, tiled=True)  11.2 us
    pallas_call x1, Pallas kernels, shards(): pl.pallas_call(cross_kernel, out_shape=(jax.ShapeDtypeStruct((2, HD, 1024...  9.18 us
    all_to_all x1, starting transfers between devices, shards(): pieces = lax.all_to_all(partial, ring, 0, 0, tiled=True)  8.83 us
    ppermute x1, starting transfers between devices, shards(): vb = lax.ppermute(va, 'c', swap)  5.45 us
    ppermute x1, starting transfers between devices, shards(): kvb = lax.ppermute(kva, 'c', swap)  4.02 us
  transfers between devices with their start and end apart: 6, of which 4 were waited for; matrix products, arithmetic and copies ran while one was open for 3% of the time, Pallas kernels for 7%

profile of v1, /device:TPU:193, one launch (start us, length us, event | category | flops | bytes accessed | tf_op | source)
XLA Modules:
  0.0 131.4 jit_solution(918710584048639033)
XLA Ops:
  7.2 0.0 copy-start.6
  7.2 0.0 copy-start.7
  7.2 0.0 copy-start.8
  7.2 0.0 copy-start.2
  7.2 0.0 copy-start.1
  7.2 0.0 all-gather.2.cloned.1.call-start
  7.3 1.0 copy.11
  8.3 1.3 collective-permute-start
  9.6 1.0 stack_reshape.4
  10.6 2.2 %collective-permute-done = bf16[128,512]{1,0:T(8,128)(2,1)S(1)} collective-permute-done((bf16[128,512]{1,0:T(8,128)(2,1)S(1)}, bf16[128,512]{1,0:T(8,128)(2,1)S(1)}, u32[]{:S(2)}, u32[]{:S(2)}) %collective-permute-start) | collective-permute-done | bytes 131104 | tf_op jit(solution)/shard_map/ppermute | solution.py:171
  12.7 0.7 maximum_select_fusion
  13.4 0.0 all-gather.2.cloned.1.call-update
  13.5 0.7 copy.12
  14.2 27.9 %all_to_all.10 = bf16[64,8,512]{2,1,0:T(8,128)(2,1)S(1)} all-to-all(bf16[64,8,512]{2,1,0:T(8,128)(2,1)S(1)} %broadcast_in_dim.21), channel_id=1, replica_groups=mesh['y'=4,'z'=8,'x'=2,'c'=2,'t'=2] {'y','z','x'}, dimensions={0} | all-to-all | bytes 1048576 | tf_op jit(solution)/shard_map/all_to_all | solution.py:178
  42.1 5.5 %collective-permute-start.2 = (bf16[512,512]{1,0:T(8,128)(2,1)S(1)}, bf16[512,512]{1,0:T(8,128)(2,1)S(1)}, u32[]{:S(2)}, u32[]{:S(2)}) collective-permute-start(bf16[512,512]{1,0:T(8,128)(2,1)S(1)} %bitcast.22), channel_id=1, source_target_pairs={{0,2},{2,0},{1,3},{3,1},{4,6},{6,4},{5,7},{7,5},{8,10},{10,8},{9,1... | collective-permute-start | bytes 1572872 | tf_op jit(solution)/shard_map/ppermute | solution.py:181
  47.6 0.0 copy-done.6
  47.6 0.1 reshape.49
  47.6 0.0 copy-done.7
  47.6 0.2 reduce-window.4
  47.8 0.0 copy-done.8
  47.8 0.1 tanh.19
  47.9 0.1 tile.9.gate_row_ref
  48.1 0.1 pad_add_fusion.1.info_ref
  48.1 11.2 %all-gather.2.cloned.1.call-done.kva_ref = bf16[2048,512]{1,0:T(8,128)(2,1)} async-done(((bf16[256,512]{1,0:T(8,128)(2,1)}), bf16[2048,512]{1,0:T(8,128)(2,1)}) %all-gather.2.cloned.1.call-update) | async-done | bytes 2097168 | tf_op jit(solution)/shard_map/all_gather | solution.py:173
  59.3 4.0 %collective-permute-start.1 = (bf16[2048,512]{1,0:T(8,128)(2,1)}, bf16[2048,512]{1,0:T(8,128)(2,1)}, u32[]{:S(2)}, u32[]{:S(2)}) collective-permute-start(bf16[2048,512]{1,0:T(8,128)(2,1)} %all-gather.2.cloned.1.call-done.kva_ref), channel_id=1, source_target_pairs={{0,2},{2,0},{1,3},{3,1},{4,6},{6,4},{5,7},{7,5},{8,10},{10,8},{9,1... | collective-permute-start | bytes 6291464 | tf_op jit(solution)/shard_map/ppermute | solution.py:174
  63.4 0.0 collective-permute-done.2.vb_ref
  63.4 0.1 broadcast_in_dim.19.gate_col_ref
  63.4 0.0 copy-done.2
  63.4 0.0 copy-done.1
  63.4 9.2 %cross_attention.1 = (f32[2,128,1024]{2,1,0:T(8,128)S(1)}, bf16[128,16,128]{2,1,0:T(8,128)(2,1)}, f32[512,512]{1,0:T(8,128)S(1)}, bf16[512,512]{1,0:T(8,128)(2,1)S(1)}) custom-call(s32[13]{0:T(128)S(1)} %pad_add_fusion.1.info_ref, bf16[128,16,128]{2,1,0:T(8,128)(2,1)S(1)} %bitcast.24, bf16[128,16,128]{2,1,0:T(8,128)(2,1)S(1)} %bitcast.25, ...), custom_call_target="tpu_custom_call" | custom-call | flops 3221225472 | bytes 6291456 | tf_op jit(solution)/shard_map/cross_attention/pallas_call | solution.py:192
  72.6 0.0 copy-start.4
  72.6 1.0 copy-done.4
  73.6 0.0 copy-start
  73.6 0.0 copy-start.3
  73.6 0.0 collective-permute-start.3
  73.6 1.9 %collective-permute-done.3 = bf16[512,512]{1,0:T(8,128)(2,1)S(1)} collective-permute-done((bf16[512,512]{1,0:T(8,128)(2,1)S(1)}, bf16[512,512]{1,0:T(8,128)(2,1)S(1)}, u32[]{:S(2)}, u32[]{:S(2)}) %collective-permute-start.3) | collective-permute-done | bytes 524320 | tf_op jit(solution)/shard_map/ppermute | solution.py:210
  75.5 1.0 fusion
  76.5 8.8 %all-to-all-start.1 = ((bf16[64,8,512]{2,1,0:T(8,128)(2,1)}), bf16[64,8,512]{2,1,0:T(8,128)(2,1)S(1)}, u32[]{:S(2)}, u32[]{:S(2)}) async-start(bf16[64,8,512]{2,1,0:T(8,128)(2,1)} %fusion), calls=%async_computation.1 | async-start | bytes 1048576 | tf_op jit(solution)/shard_map/all_to_all | solution.py:212
  85.3 0.1 pad_add_fusion.info_ref
  85.4 16.0 %all-to-all-done.1 = bf16[64,8,512]{2,1,0:T(8,128)(2,1)S(1)} async-done(((bf16[64,8,512]{2,1,0:T(8,128)(2,1)}), bf16[64,8,512]{2,1,0:T(8,128)(2,1)S(1)}, u32[]{:S(2)}, u32[]{:S(2)}) %all-to-all-start.1) | async-done | bytes 524320 | tf_op jit(solution)/shard_map/all_to_all | solution.py:212
  101.3 0.1 convert_reduce_fusion
  101.4 0.6 reshape.52
  102.1 0.0 collective-permute-done.1.kvb_ref
  102.1 0.0 copy-done
  102.1 0.0 copy-done.3
  102.1 0.0 copy-start.5
  102.1 1.2 copy-done.5
  103.3 21.2 %self_attention.1 = bf16[128,16,128]{2,1,0:T(8,128)(2,1)} custom-call(s32[2]{0:T(128)S(1)} %pad_add_fusion.info_ref, bf16[128,16,128]{2,1,0:T(8,128)(2,1)S(1)} %bitcast.26, bf16[2048,512]{1,0:T(8,128)(2,1)S(1)} %copy-done, bf16[2048,512]{1,0:T(8,128)(2,1)} %collective-permute-done.1.kvb_ref, f32[2,128,1024]{2,1,0:T(8,128)S(1)} %copy-done.5), custom_call_target="tpu_custom_call" | custom-call | flops 4294967296 | bytes 6291456 | tf_op jit(solution)/shard_map/self_attention/pallas_call | solution.py:215
  (4 shorter events, 0.1 us)
Async XLA Ops:
  7.2 40.4 %copy-start.6 = (s32[2,4]{1,0:T(2,128)S(1)}, s32[2,4]{1,0:T(2,128)}, u32[]{:S(2)}) copy-start(s32[2,4]{1,0:T(2,128)} %param.13) | copy-start | bytes 100
  7.2 40.5 %copy-start.7 = (s32[4]{0:T(128)S(1)}, s32[4]{0:T(128)}, u32[]{:S(2)}) copy-start(s32[4]{0:T(128)} %param.14) | copy-start | bytes 52
  7.2 40.6 %copy-start.8 = (f32[1,16]{1,0:T(1,128)S(1)}, f32[1,16]{1,0:T(1,128)}, u32[]{:S(2)}) copy-start(f32[1,16]{1,0:T(1,128)} %param.12) | copy-start | bytes 196
  7.2 56.2 %copy-start.2 = (bf16[1,128,16,128]{3,2,1,0:T(8,128)(2,1)S(1)}, bf16[1,128,16,128]{3,2,1,0:T(8,128)(2,1)}, u32[]{:S(2)}) copy-start(bf16[1,128,16,128]{3,2,1,0:T(8,128)(2,1)} %param.15) | copy-start | bytes 1572868
  7.2 56.2 %copy-start.1 = (bf16[1,128,16,128]{3,2,1,0:T(8,128)(2,1)S(1)}, bf16[1,128,16,128]{3,2,1,0:T(8,128)(2,1)}, u32[]{:S(2)}) copy-start(bf16[1,128,16,128]{3,2,1,0:T(8,128)(2,1)} %param.10) | copy-start | bytes 1572868
  7.2 52.1 %all-gather.2.cloned.1.call-start = ((), (), s32[]{:S(2)}) async-start(), calls=%async_computation.2 | async-start | bytes 2359296 | tf_op jit(solution)/shard_map/all_gather | solution.py:173
  8.3 4.5 %collective-permute-start = (bf16[128,512]{1,0:T(8,128)(2,1)S(1)}, bf16[128,512]{1,0:T(8,128)(2,1)S(1)}, u32[]{:S(2)}, u32[]{:S(2)}) collective-permute-start(bf16[128,512]{1,0:T(8,128)(2,1)S(1)} %bitcast.30), channel_id=1, source_target_pairs={{0,4},{4,0},{1,5},{5,1},{2,6},{6,2},{3,7},{7,3},{8,12},{12,8},{9,1... | collective-permute-start | bytes 393224 | tf_op jit(solution)/shard_map/ppermute | solution.py:171
  42.1 21.2 %collective-permute-start.2 = (bf16[512,512]{1,0:T(8,128)(2,1)S(1)}, bf16[512,512]{1,0:T(8,128)(2,1)S(1)}, u32[]{:S(2)}, u32[]{:S(2)}) collective-permute-start(bf16[512,512]{1,0:T(8,128)(2,1)S(1)} %bitcast.22), channel_id=1, source_target_pairs={{0,2},{2,0},{1,3},{3,1},{4,6},{6,4},{5,7},{7,5},{8,10},{10,8},{9,1... | collective-permute-start | bytes 1572872 | tf_op jit(solution)/shard_map/ppermute | solution.py:181
  59.3 42.7 %collective-permute-start.1 = (bf16[2048,512]{1,0:T(8,128)(2,1)}, bf16[2048,512]{1,0:T(8,128)(2,1)}, u32[]{:S(2)}, u32[]{:S(2)}) collective-permute-start(bf16[2048,512]{1,0:T(8,128)(2,1)} %all-gather.2.cloned.1.call-done.kva_ref), channel_id=1, source_target_pairs={{0,2},{2,0},{1,3},{3,1},{4,6},{6,4},{5,7},{7,5},{8,10},{10,8},{9,1... | collective-permute-start | bytes 6291464 | tf_op jit(solution)/shard_map/ppermute | solution.py:174
  72.6 1.0 copy-start.4
  73.6 28.5 %copy-start = (bf16[2048,512]{1,0:T(8,128)(2,1)S(1)}, bf16[2048,512]{1,0:T(8,128)(2,1)}, u32[]{:S(2)}) copy-start(bf16[2048,512]{1,0:T(8,128)(2,1)} %all-gather.2.cloned.1.call-done.kva_ref) | copy-start | bytes 6291460
  73.6 28.5 %copy-start.3 = (bf16[1,128,16,128]{3,2,1,0:T(8,128)(2,1)S(1)}, bf16[1,128,16,128]{3,2,1,0:T(8,128)(2,1)}, u32[]{:S(2)}) copy-start(bf16[1,128,16,128]{3,2,1,0:T(8,128)(2,1)} %param.8) | copy-start | bytes 1572868
  73.6 1.9 %collective-permute-start.3 = (bf16[512,512]{1,0:T(8,128)(2,1)S(1)}, bf16[512,512]{1,0:T(8,128)(2,1)S(1)}, u32[]{:S(2)}, u32[]{:S(2)}) collective-permute-start(bf16[512,512]{1,0:T(8,128)(2,1)S(1)} %get-tuple-element.10), channel_id=1, source_target_pairs={{0,2},{2,0},{1,3},{3,1},{4,6},{6,4},{5,7},{7,5},{8,10},{10,8},{9,1... | collective-permute-start | bytes 1572872 | tf_op jit(solution)/shard_map/ppermute | solution.py:210
  76.5 24.9 %all-to-all-start.1 = ((bf16[64,8,512]{2,1,0:T(8,128)(2,1)}), bf16[64,8,512]{2,1,0:T(8,128)(2,1)S(1)}, u32[]{:S(2)}, u32[]{:S(2)}) async-start(bf16[64,8,512]{2,1,0:T(8,128)(2,1)} %fusion), calls=%async_computation.1 | async-start | bytes 1048576 | tf_op jit(solution)/shard_map/all_to_all | solution.py:212
  102.1 1.2 copy-start.5
Sparse Core Ops, SparseCore 0:
  13.6 45.6 all-gather.1

commit v2 on v1

v2 whole, which is shorter than its diff:
```python
import math

import jax
import jax.numpy as jnp
from jax import lax
from jax.experimental import pallas as pl
from jax.experimental.pallas import tpu as pltpu
from jax.sharding import Mesh, PartitionSpec as P

IMAGES = 4
BLOCK = 64
HD = 128
NEG = -1e30
F32 = jnp.float32
BF16 = jnp.bfloat16
SCALE = 1.0 / math.sqrt(HD)
SCALE2 = SCALE / math.log(2.0)
NT = (((1,), (1,)), ((), ()))


def nt(a, b):
    return lax.dot_general(a, b, NT, preferred_element_type=F32)


def nn(a, b):
    return jnp.dot(a, b, preferred_element_type=F32)


def flip(a):
    return jnp.transpose(a.astype(F32), (1, 0)).astype(a.dtype)


def cross_kernel(
    image_ref,
    mask_ref,
    cq_ref,
    cot_ref,
    gate_ref,
    va_ref,
    vb_ref,
    out_ref,
    gq_ref,
    ga_ref,
    gb_ref,
):
    h = pl.program_id(0)
    core = lax.axis_index("c")
    half = va_ref.shape[0]
    count = 2 * half
    rows = cq_ref.shape[0] * 8
    lane = lax.broadcasted_iota(jnp.int32, (1, count), 1)
    which = jnp.where(lane < half, core, 1 - core)
    part = lane % half // 8
    token = (((part // 16 * 8 + part % 8) * 2 + part // 8 % 2) * 2 + which) * 8 + lane % 8
    live = []
    for rb in range(2):
        on = jnp.zeros((1, count), jnp.int32) + mask_ref[rb, 0]
        bound = 0
        for k in range(IMAGES - 1):
            bound = bound + image_ref[k]
            on = jnp.where(token >= bound, mask_ref[rb, k + 1], on)
        live.append(jnp.broadcast_to(jnp.where(on == 1, 0.0, NEG), (rows // 2, count)))
    bias = jnp.concatenate(live, axis=0)

    keys = jnp.concatenate([va_ref[:, :HD], vb_ref[:, :HD]], axis=0)
    values = jnp.concatenate([va_ref[:, HD:], vb_ref[:, HD:]], axis=0)
    head = lax.broadcasted_iota(jnp.int32, (8, 16), 0) + h * 8
    chosen = lax.broadcasted_iota(jnp.int32, (8, 16), 1) == head
    gates = jnp.where(chosen, jnp.broadcast_to(gate_ref[...], (8, 16)), 0.0)
    gate = jnp.tanh(jnp.broadcast_to(jnp.sum(gates, axis=1, keepdims=True), (8, HD)))

    q = cq_ref[...].reshape(rows, HD)
    go = (cot_ref[...].astype(F32) * gate[None]).astype(BF16).reshape(rows, HD)
    s = nt(q, keys) * SCALE2 + bias
    top = jnp.max(s, axis=1, keepdims=True)
    top = jnp.where(top < 0.5 * NEG, 0.0, top)
    p = jnp.exp2(s - top)
    pb = p.astype(BF16)
    both = nn(pb, with_ones(values))
    inv = 1.0 / jnp.maximum(both[:, HD:], 1.0)
    cross = both[:, :HD] * inv
    out_ref[...] = cross.reshape(rows // 8, 8, HD) * gate[None]
    dot = jnp.sum(go.astype(F32) * cross, axis=1, keepdims=True)
    ds = (p * (nt(go, values) - dot)).astype(BF16)
    gq_ref[...] = (nn(ds, keys) * (inv * SCALE)).reshape(rows // 8, 8, HD).astype(BF16)
    qs = (q.astype(F32) * (inv * SCALE)).astype(BF16)
    gs = (go.astype(F32) * inv).astype(BF16)
    dk = jnp.transpose(nn(flip(qs), ds), (1, 0))
    dv = jnp.transpose(nn(flip(gs), pb), (1, 0))
    ga_ref[:, :HD] = dk[:half]
    ga_ref[:, HD:] = dv[:half]
    gb_ref[:, :HD] = dk[half:].astype(BF16)
    gb_ref[:, HD:] = dv[half:].astype(BF16)


LOCAL = 512
TILE = 256


def attend(q, keys, values, limit, top, total, acc):
    s = nt(q, keys) * SCALE2
    if limit is not None:
        s = jnp.where(limit, s, NEG)
    new = jnp.maximum(top, jnp.broadcast_to(jnp.max(s, axis=1, keepdims=True), top.shape))
    factor = jnp.exp2(top - new)
    p = jnp.exp2(s - jnp.tile(new, (1, keys.shape[0] // HD))).astype(BF16)
    both = nn(p, values)
    return new, total * factor + both[:, HD:], acc * factor + both[:, :HD]


def with_ones(values):
    return jnp.concatenate([values, jnp.ones_like(values)], axis=1)


def fetch_blocks(own_refs, other_refs, kv_ref, sems):
    half = LOCAL // 2
    for i, pair in enumerate(zip(own_refs, other_refs)):
        for side, source in enumerate(pair):
            target = kv_ref.at[i, pl.ds(side * half, half), :]
            pltpu.make_async_copy(source, target, sems.at[i, side]).start()


def wait_block(kv_ref, sems, block):
    half = LOCAL // 2
    for side in range(2):
        place = kv_ref.at[block, pl.ds(side * half, half), :]
        pltpu.make_async_copy(place, place, sems.at[block, side]).wait()


def blend(q_own, kv_ref, block, top_ref, sum_ref, acc_ref):
    for h in range(2):
        lane = h * 2 * HD
        keys = kv_ref[block, :, lane : lane + HD]
        values = with_ones(kv_ref[block, :, lane + HD : lane + 2 * HD])
        for t in range(1024 // TILE):
            cols = slice(t * TILE, (t + 1) * TILE)
            state = top_ref[h, cols, :], sum_ref[h, cols, :], acc_ref[h, cols, :]
            state = attend(q_own[h, cols, :], keys, values, None, *state)
            top_ref[h, cols, :], sum_ref[h, cols, :], acc_ref[h, cols, :] = state


NEAR = 7
FAR = 1


def near_kernel(*refs):
    own_refs, other_refs = refs[:NEAR], refs[NEAR : 2 * NEAR]
    q_ref, acc_out, lse_out, kv_ref, acc_ref, top_ref, sum_ref, q_own, sems = refs[2 * NEAR :]
    fetch_blocks(own_refs, other_refs, kv_ref, sems)
    for h in range(2):
        q_own[h] = q_ref[:, h * 8 : h * 8 + 8, :].reshape(1024, HD)
    z = lax.axis_index("z")
    core = lax.axis_index("c")
    half = LOCAL // 2
    key = lax.broadcasted_iota(jnp.int32, (TILE, LOCAL), 1)
    from_core = jnp.where(key < half, core, 1 - core)
    place = key % half
    place = (place // 128) * 256 + from_core * 128 + place % 128
    row = lax.broadcasted_iota(jnp.int32, (TILE, LOCAL), 0) // 8
    row = row + lax.axis_index("x") * 256 + core * 128
    start = jnp.full((TILE, HD), NEG, F32)
    zero = jnp.zeros((TILE, HD), F32)
    wait_block(kv_ref, sems, 0)
    for h in range(2):
        lane = h * 2 * HD
        keys = kv_ref[0, :, lane : lane + HD]
        values = with_ones(kv_ref[0, :, lane + HD : lane + 2 * HD])
        for t in range(1024 // TILE):
            cols = slice(t * TILE, (t + 1) * TILE)
            limit = place <= row + t * (TILE // 8)
            state = attend(q_own[h, cols, :], keys, values, limit, start, zero, zero)
            top_ref[h, cols, :], sum_ref[h, cols, :], acc_ref[h, cols, :] = state

    @pl.loop(1, NEAR)
    def _(block):
        wait_block(kv_ref, sems, block)
        step = (block + 1) // 2

        @pl.when(jnp.where(block % 2 == 1, z >= step, z + step >= 8))
        def _():
            blend(q_own, kv_ref, block, top_ref, sum_ref, acc_ref)

    acc_out[...] = acc_ref[...] / sum_ref[...]
    lse_out[...] = top_ref[...] + jnp.log2(sum_ref[...])


def far_kernel(*refs):
    own_ref, other_ref, q_ref, acc_in, lse_in, cross_ref, out_ref = refs[:7]
    kv_ref, acc_ref, top_ref, sum_ref, q_own, sems = refs[7:]
    fetch_blocks([own_ref], [other_ref], kv_ref, sems)
    for h in range(2):
        q_own[h] = q_ref[:, h * 8 : h * 8 + 8, :].reshape(1024, HD)
    acc_ref[...] = acc_in[...]
    top_ref[...] = lse_in[...]
    sum_ref[...] = jnp.ones_like(sum_ref)
    wait_block(kv_ref, sems, 0)

    @pl.when(lax.axis_index("z") >= 4)
    def _():
        blend(q_own, kv_ref, 0, top_ref, sum_ref, acc_ref)

    for h in range(2):
        mixed = (acc_ref[h] / sum_ref[h]).reshape(2 * BLOCK, 8, HD)
        out_ref[:, h * 8 : h * 8 + 8, :] = (mixed + cross_ref[:, h * 8 : h * 8 + 8, :]).astype(BF16)


def sum_kernel(pieces_ref, out_ref):
    total = jnp.sum(pieces_ref[...].astype(F32), axis=0)
    for h in range(2):
        out_ref[:, h, :] = total[:, h * 2 * HD : (h + 1) * 2 * HD]


def pair_kernel(own_ref, other_ref, out_ref):
    x = lax.axis_index("x")
    rows = own_ref.shape[0]
    out_ref[pl.ds(pl.multiple_of(x * rows, rows), rows), :] = own_ref[...]
    out_ref[pl.ds(pl.multiple_of((1 - x) * rows, rows), rows), :] = other_ref[...]


def pick_kernel(first_ref, second_ref, out_ref):
    core = lax.axis_index("c")

    @pl.when(core == 0)
    def _():
        out_ref[...] = first_ref[...]

    @pl.when(core == 1)
    def _():
        out_ref[...] = second_ref[...]


def spec():
    return pl.BlockSpec(memory_space=pltpu.VMEM)


def shards(
    self_q, self_kv, cross_q, vision_kv, cross_gate, cross_mask, image_tokens, out_cotangent
):
    swap = [(0, 1), (1, 0)]
    up = [(i, (i + 1) % 8) for i in range(8)]
    down = [(i, (i + 7) % 8) for i in range(8)]
    ring = ("y", "x", "z")
    parts = lax.axis_size(ring)
    tokens = parts * 8
    tie = lax.optimization_barrier

    image = jnp.broadcast_to(vision_kv.reshape(1, 8, 4 * HD), (8, 8, 4 * HD))
    kv = self_kv.reshape(128, 4 * HD)
    other = lax.ppermute(kv, "x", swap)
    column = lax.all_to_all(image, "z", 0, 0, tiled=True).reshape(1, 64, 4 * HD)
    column, kv, other = tie((column, kv, other))
    pair = pl.pallas_call(
        pair_kernel,
        out_shape=jax.ShapeDtypeStruct((256, 4 * HD), BF16),
        in_specs=[spec()] * 2,
        out_specs=spec(),
        compiler_params=pltpu.CompilerParams(vmem_limit_bytes=4 << 20),
        name="pair",
    )(kv, other)
    va = lax.all_to_all(
        jnp.broadcast_to(column, (8, 64, 4 * HD)), ("y", "x"), 0, 0, tiled=True
    ).reshape(tokens, 4 * HD)
    up1, down1 = lax.ppermute(pair, "z", up), lax.ppermute(pair, "z", down)
    pair_c = lax.ppermute(pair, "c", swap)

    va, up1, down1, pair_c = tie((va, up1, down1, pair_c))
    vb = lax.ppermute(va, "c", swap)
    up2, down2 = lax.ppermute(up1, "z", up), lax.ppermute(down1, "z", down)
    up1c, down1c = lax.ppermute(up1, "c", swap), lax.ppermute(down1, "c", swap)

    smem = pl.BlockSpec(memory_space=pltpu.SMEM)
    by_head = pl.BlockSpec((128, 8, HD), lambda h: (0, h, 0))
    by_lane = pl.BlockSpec((tokens, 2 * HD), lambda h: (0, h))
    cross, grad_q, grad_own, grad_other = pl.pallas_call(
        cross_kernel,
        grid=(2,),
        out_shape=(
            jax.ShapeDtypeStruct((128, 16, HD), F32),
            jax.ShapeDtypeStruct((128, 16, HD), BF16),
            jax.ShapeDtypeStruct((tokens, 4 * HD), F32),
            jax.ShapeDtypeStruct((tokens, 4 * HD), BF16),
        ),
        in_specs=[smem, smem, by_head, by_head, spec(), by_lane, by_lane],
        out_specs=[by_head, by_head, by_lane, by_lane],
        compiler_params=pltpu.CompilerParams(vmem_limit_bytes=40 << 20),
        cost_estimate=pl.CostEstimate(
            flops=6 * 2 * 2 * 1024 * 1024 * 128, bytes_accessed=6 << 20, transcendentals=2 << 20
        ),
        name="cross_attention",
    )(image_tokens, cross_mask, cross_q[0], out_cotangent[0], cross_gate, va, vb)

    grad_other, up1c, down1c, up2, down2 = tie((grad_other, up1c, down1c, up2, down2))
    received = lax.ppermute(grad_other, "c", swap)
    up3, down3 = lax.ppermute(up2, "z", up), lax.ppermute(down2, "z", down)
    up2c, down2c = lax.ppermute(up2, "c", swap), lax.ppermute(down2, "c", swap)
    partial = (grad_own + received.astype(F32)).astype(BF16).reshape(parts, 8, 4 * HD)
    partial, up2c, down2c = tie((partial, up2c, down2c))
    pieces = lax.all_to_all(partial, ring, 0, 0, tiled=True)

    hbm = pl.BlockSpec(memory_space=pl.ANY)

    def scratch(count):
        return [
            pltpu.VMEM((count, LOCAL, 4 * HD), BF16),
            pltpu.VMEM((2, 1024, HD), F32),
            pltpu.VMEM((2, 1024, HD), F32),
            pltpu.VMEM((2, 1024, HD), F32),
            pltpu.VMEM((2, 1024, HD), BF16),
            pltpu.SemaphoreType.DMA((count, 2)),
        ]

    def cost(count):
        return pl.CostEstimate(
            flops=count * 2 * 2 * 2 * 512 * 1024 * 128,
            bytes_accessed=6 << 20,
            transcendentals=count << 20,
        )

    split = pl.pallas_call(
        pick_kernel,
        out_shape=jax.ShapeDtypeStruct(up3.shape, BF16),
        in_specs=[spec()] * 2,
        out_specs=spec(),
        compiler_params=pltpu.CompilerParams(vmem_limit_bytes=4 << 20),
        name="pick",
    )(up3, down3)
    halves = [
        (zi * 2 + ci, (zi + (1 if ci == 0 else 7)) % 8 * 2 + ci)
        for zi in range(8)
        for ci in range(2)
    ]
    last = lax.ppermute(split, ("z", "c"), halves)
    up3c, down3c = lax.ppermute(up3, "c", swap), lax.ppermute(down3, "c", swap)
    near = [pair, up1, down1, up2, down2, up3, down3]
    near += [pair_c, up1c, down1c, up2c, down2c, up3c, down3c]
    acc, lse = pl.pallas_call(
        near_kernel,
        out_shape=(jax.ShapeDtypeStruct((2, 1024, HD), F32),) * 2,
        in_specs=[hbm] * (2 * NEAR) + [spec()],
        out_specs=[spec()] * 2,
        scratch_shapes=scratch(NEAR),
        compiler_params=pltpu.CompilerParams(vmem_limit_bytes=24 << 20),
        cost_estimate=cost(NEAR),
        name="self_near",
    )(*near, self_q[0])

    last, acc = tie((last, acc))
    last_c = lax.ppermute(last, "c", swap)
    mixed = pl.pallas_call(
        far_kernel,
        out_shape=jax.ShapeDtypeStruct((128, 16, HD), BF16),
        in_specs=[hbm] * (2 * FAR) + [spec()] * 4,
        out_specs=spec(),
        scratch_shapes=scratch(FAR),
        compiler_params=pltpu.CompilerParams(vmem_limit_bytes=24 << 20),
        cost_estimate=cost(FAR),
        name="self_far",
    )(last, last_c, self_q[0], acc, lse, cross)

    pieces, mixed = tie((pieces, mixed))
    image_grads = pl.pallas_call(
        sum_kernel,
        out_shape=jax.ShapeDtypeStruct((8, 2, 2 * HD), F32),
        in_specs=[spec()],
        out_specs=spec(),
        name="sum_pieces",
    )(pieces)
    return (mixed[None], grad_q[None], image_grads)


def solution(mesh):
    fine = Mesh(mesh.devices.reshape(4, 8, 2, 2, 2), ("y", "z", "x", "c", "t"))
    rows = P("y", ("z", "x", "c"), "t", None)
    image = P(("y", "z", "x", "c"), "t", None)
    return jax.shard_map(
        shards,
        mesh=fine,
        in_specs=(rows, rows, rows, image, P("y", "t"), P(("z", "x", "c"), None), P(), rows),
        out_specs=(rows, rows, image),
        check_vma=False,
    )
```

time: 132 us -> 82 us (0.62)
  the two profiles are of different devices: /device:TPU:193 before, /device:TPU:4 now
where the time goes in v2:
time: 82 us; the launch traced here: 80.5 us
  starting transfers between devices  26.5 us (32%)
  waiting for transfers between devices  18 us (22%)
  blocking collectives  16.6 us (20%)
  Pallas kernels  14.4 us (18%)
  local copies, waits for them, and re-layouts  3.18 us (4%)
  other arithmetic  0.97 us (1%)
  between operations  0.87 us (1%)
    all_to_all x1, blocking collectives, shards(): column = lax.all_to_all(image, 'z', 0, 0, tiled=True).reshape(1, 64, 4 * HD)  16.6 us
    ppermute x1, waiting for transfers between devices, shards(): last = lax.ppermute(split, ('z', 'c'), halves)  11.8 us
    pallas_call x1, Pallas kernels, shards(): pl.pallas_call(cross_kernel, grid=(2,), out_shape=(jax.ShapeDtypeStruct((...  8.53 us
    all_to_all x1, starting transfers between devices, shards(): pieces = lax.all_to_all(partial, ring, 0, 0, tiled=True)  7.25 us
    all_to_all x1, starting transfers between devices, shards(): lax.all_to_all(jnp.broadcast_to(column, (8, 64, 4 * HD)), ('y', 'x'), 0,...  4.87 us
    ppermute x2, waiting for transfers between devices, shards(): up1, down1 = (lax.ppermute(pair, 'z', up), lax.ppermute(pair, 'z', down))  4.34 us
    ppermute x2, starting transfers between devices, shards(): up1, down1 = (lax.ppermute(pair, 'z', up), lax.ppermute(pair, 'z', down))  3.31 us
    ppermute x2, starting transfers between devices, shards(): up2, down2 = (lax.ppermute(up1, 'z', up), lax.ppermute(down1, 'z', down))  3.24 us
  transfers between devices with their start and end apart: 20, of which 4 were waited for; matrix products, arithmetic and copies ran while one was open for 1% of the time, Pallas kernels for 16%

profile of v2, /device:TPU:4, one launch (start us, length us, event | category | flops | bytes accessed | tf_op | source)
XLA Modules:
  0.0 80.5 jit_solution(12268593650435562123)
XLA Ops:
  0.6 0.0 copy-start.12
  0.6 0.9 %copy.12 = bf16[16,8,2,256]{3,1,2,0:T(8,128)(2,1)S(1)} copy(bf16[16,8,2,256]{3,2,1,0:T(2,128)(2,1)} %bitcast.25) | data formatting | bytes 262144
  1.6 1.3 %collective-permute-start = (bf16[128,512]{1,0:T(8,128)(2,1)S(1)}, bf16[128,512]{1,0:T(8,128)(2,1)S(1)}, u32[]{:S(2)}, u32[]{:S(2)}) collective-permute-start(bf16[128,512]{1,0:T(8,128)(2,1)S(1)} %bitcast.19), channel_id=1, source_target_pairs={{0,4},{4,0},{1,5},{5,1},{2,6},{6,2},{3,7},{7,3},{8,12},{12,8},{9,1... | collective-permute-start | bytes 393224 | tf_op jit(solution)/shard_map/ppermute | solution.py:249
  2.9 0.0 copy-done.12
  2.9 16.6 %all_to_all.15 = bf16[8,8,512]{2,1,0:T(8,128)(2,1)S(1)} all-to-all(bf16[8,8,512]{2,1,0:T(8,128)(2,1)S(1)} %broadcast_in_dim.21), channel_id=1, replica_groups=mesh['y'=4,'z'=8,'x'=2,'c'=2,'t'=2] {'z'}, dimensions={0} | all-to-all | bytes 131072 | tf_op jit(solution)/shard_map/all_to_all | solution.py:250
  19.5 0.0 collective-permute-done.other_ref
  19.5 0.8 %broadcast_in_dim.23 = bf16[8,64,512]{2,1,0:T(8,128)(2,1)} broadcast(bf16[64,512]{1,0:T(8,128)(2,1)S(1)} %bitcast.24), dimensions={1,2} | broadcast | bytes 589824 | tf_op jit(solution)/shard_map/broadcast_in_dim | solution.py:261
  20.4 4.9 %all-to-all-start.1 = ((bf16[8,64,512]{2,1,0:T(8,128)(2,1)}), bf16[8,64,512]{2,1,0:T(8,128)(2,1)S(1)}, u32[]{:S(2)}, u32[]{:S(2)}) async-start(bf16[8,64,512]{2,1,0:T(8,128)(2,1)} %broadcast_in_dim.23), calls=%async_computation.1 | async-start | bytes 1048576 | tf_op jit(solution)/shard_map/all_to_all | solution.py:260
  25.2 0.0 copy-start.11
  25.3 0.6 collective-permute-start.1
  25.9 2.7 %collective-permute-start.2 = (bf16[256,512]{1,0:T(8,128)(2,1)S(1)}, bf16[256,512]{1,0:T(8,128)(2,1)S(1)}, u32[]{:S(2)}, u32[]{:S(2)}) collective-permute-start(bf16[256,512]{1,0:T(8,128)(2,1)S(1)} %pair.1.refs_0_), channel_id=1, source_target_pairs={{0,56},{8,0},{16,8},{24,16},{32,24},{40,32},{48,40},{56,48},{1,57}... | collective-permute-start | bytes 786440 | tf_op jit(solution)/shard_map/ppermute | solution.py:263
  28.6 0.0 collective-permute-start.3
  28.6 4.3 %collective-permute-done.1.refs_1_ = bf16[256,512]{1,0:T(8,128)(2,1)S(1)} collective-permute-done((bf16[256,512]{1,0:T(8,128)(2,1)S(1)}, bf16[256,512]{1,0:T(8,128)(2,1)S(1)}, u32[]{:S(2)}, u32[]{:S(2)}) %collective-permute-start.1) | collective-permute-done | bytes 262176 | tf_op jit(solution)/shard_map/ppermute | solution.py:263
  32.9 0.0 collective-permute-done.2.refs_2_
  32.9 0.0 collective-permute-done.3.refs_7_
  32.9 0.7 copy-done.3
  33.7 0.3 all-to-all-done.1
  33.9 0.0 collective-permute-start.4
  33.9 0.5 collective-permute-start.5
  34.4 0.6 collective-permute-start.7
  35.0 0.0 collective-permute-start.6
  35.0 2.7 %collective-permute-start.8 = (bf16[256,512]{1,0:T(8,128)(2,1)S(1)}, bf16[256,512]{1,0:T(8,128)(2,1)}, u32[]{:S(2)}, u32[]{:S(2)}) collective-permute-start(bf16[256,512]{1,0:T(8,128)(2,1)S(1)} %collective-permute-done.2.refs_2_), channel_id=1, source_target_pairs={{0,56},{8,0},{16,8},{24,16},{32,24},{40,32},{48,40},{56,48},{1,57}... | collective-permute-start | bytes 786440 | tf_op jit(solution)/shard_map/ppermute | solution.py:268
  37.7 0.0 collective-permute-done.4.vb_ref
  37.7 0.0 copy-done.2
  37.7 0.0 copy-done.1
  37.7 0.0 copy-done.11
  37.7 0.7 copy-done.9
  38.3 0.0 copy-done.10
  38.3 8.5 %cross_attention.1 = (f32[128,16,128]{2,1,0:T(8,128)S(1)}, bf16[128,16,128]{2,1,0:T(8,128)(2,1)}, f32[512,512]{1,0:T(8,128)S(1)}, bf16[512,512]{1,0:T(8,128)(2,1)S(1)}) custom-call(s32[4]{0:T(128)S(1)} %copy-done.10, s32[2,4]{1,0:T(2,128)S(1)} %copy-done.9, bf16[128,16,128]{2,1,0:T(8,128)(2,1)S(1)} %bitcast.21, bf16[128,16,128]{2,1,0:T(8,128)(2,1)S(1)} %bitcast.22, ...), custom_call_target="tpu_custom_call" | custom-call | flops 3221225472 | bytes 6291456 | tf_op jit(solution)/shard_map/cross_attention/pallas_call | solution.py:274
  46.9 0.0 collective-permute-done.5.refs_8_
  46.9 0.0 collective-permute-done.6.refs_9_
  46.9 0.0 copy-start.7
  46.9 0.0 collective-permute-done.7.refs_3_
  46.9 0.0 collective-permute-done.8.refs_4_
  46.9 0.3 collective-permute-start.9
  47.2 0.3 collective-permute-start.10
  47.5 0.0 collective-permute-start.12
  47.5 0.2 collective-permute-start.11
  47.7 3.0 %collective-permute-start.13 = (bf16[256,512]{1,0:T(8,128)(2,1)}, bf16[256,512]{1,0:T(8,128)(2,1)S(1)}, u32[]{:S(2)}, u32[]{:S(2)}) collective-permute-start(bf16[256,512]{1,0:T(8,128)(2,1)} %collective-permute-done.8.refs_4_), channel_id=1, source_target_pairs={{0,56},{8,0},{16,8},{24,16},{32,24},{40,32},{48,40},{56,48},{1,57}... | collective-permute-start | bytes 786440 | tf_op jit(solution)/shard_map/ppermute | solution.py:294
  50.8 0.0 collective-permute-done.9
  50.8 1.0 %fusion = bf16[64,8,512]{2,1,0:T(8,128)(2,1)} fusion(f32[512,512]{1,0:T(8,128)S(1)} %get-tuple-element.32, bf16[512,512]{1,0:T(8,128)(2,1)S(1)} %collective-permute-done.9), kind=kLoop, calls=%fused_computation.1 | loop fusion | flops 786432 | bytes 2097152 | tf_op jit(solution)/shard_map/reshape | solution.py:296
  51.7 0.0 copy-done.5
  51.7 0.0 collective-permute-done.10.refs_10_
  51.7 0.0 collective-permute-done.11.refs_11_
  51.7 0.0 copy-start.6
  51.8 7.3 %all-to-all-start.2 = ((bf16[64,8,512]{2,1,0:T(8,128)(2,1)}), bf16[64,8,512]{2,1,0:T(8,128)(2,1)}, u32[]{:S(2)}, u32[]{:S(2)}) async-start(bf16[64,8,512]{2,1,0:T(8,128)(2,1)} %fusion), calls=%async_computation.2 | async-start | bytes 1048576 | tf_op jit(solution)/shard_map/all_to_all | solution.py:298
  59.0 0.0 copy-start
  59.1 0.0 collective-permute-done.12.first_ref.refs_5_
  59.1 0.1 collective-permute-start.15
  59.2 0.0 collective-permute-done.13.second_ref.refs_6_
  59.2 0.5 collective-permute-start.16
  59.7 1.6 %collective-permute-start.14 = (bf16[256,512]{1,0:T(8,128)(2,1)S(1)}, bf16[256,512]{1,0:T(8,128)(2,1)S(1)}, u32[]{:S(2)}, u32[]{:S(2)}) collective-permute-start(bf16[256,512]{1,0:T(8,128)(2,1)S(1)} %pick.1), channel_id=1, source_target_pairs={{0,8},{2,58},{8,16},{10,2},{16,24},{18,10},{24,32},{26,18},{32,40}... | collective-permute-start | bytes 786440 | tf_op jit(solution)/shard_map/ppermute | solution.py:332
  61.3 0.0 collective-permute-done.15.refs_12_
  61.3 0.0 collective-permute-done.16.refs_13_
  61.3 0.0 copy-done.8
  61.3 0.0 copy-done
  61.3 0.0 copy-done.4
  61.3 2.7 %self_near.1 = (f32[2,1024,128]{2,1,0:T(8,128)S(1)}, f32[2,1024,128]{2,1,0:T(8,128)S(1)}) custom-call(bf16[256,512]{1,0:T(8,128)(2,1)S(1)} %pair.1.refs_0_, bf16[256,512]{1,0:T(8,128)(2,1)S(1)} %collective-permute-done.1.refs_1_, bf16[256,512]{1,0:T(8,128)(2,1)S(1)} %collective-permute-done.2.refs_2_, bf16[256,512]{1,0:T(8,128)(2,1)} %collective-permute-done.7.refs_3_, ...), custom_call_target="tpu_custom_call" | custom-call | flops 3758096384 | bytes 6291456 | tf_op jit(solution)/shard_map/self_near/pallas_call | solution.py:336
  64.1 11.8 %collective-permute-done.14.refs_0_ = bf16[256,512]{1,0:T(8,128)(2,1)S(1)} collective-permute-done((bf16[256,512]{1,0:T(8,128)(2,1)S(1)}, bf16[256,512]{1,0:T(8,128)(2,1)S(1)}, u32[]{:S(2)}, u32[]{:S(2)}) %collective-permute-start.14) | collective-permute-done | bytes 262176 | tf_op jit(solution)/shard_map/ppermute | solution.py:332
  75.9 0.0 collective-permute-start.17
  75.9 1.5 %collective-permute-done.17.refs_1_ = bf16[256,512]{1,0:T(8,128)(2,1)S(1)} collective-permute-done((bf16[256,512]{1,0:T(8,128)(2,1)S(1)}, bf16[256,512]{1,0:T(8,128)(2,1)S(1)}, u32[]{:S(2)}, u32[]{:S(2)}) %collective-permute-start.17) | collective-permute-done | bytes 262176 | tf_op jit(solution)/shard_map/ppermute | solution.py:348
  77.4 1.3 %self_far.1 = bf16[128,16,128]{2,1,0:T(8,128)(2,1)} custom-call(bf16[256,512]{1,0:T(8,128)(2,1)S(1)} %collective-permute-done.14.refs_0_, bf16[256,512]{1,0:T(8,128)(2,1)S(1)} %collective-permute-done.17.refs_1_, bf16[128,16,128]{2,1,0:T(8,128)(2,1)S(1)} %bitcast.16, f32[2,1024,128]{2,1,0:T(8,128)S(1)} %get-tuple-element.47.refs_3_, ...), custom_call_target="tpu_custom_call" | custom-call | flops 536870912 | bytes 6291456 | tf_op jit(solution)/shard_map/self_far/pallas_call | solution.py:349
  78.7 0.0 all-to-all-done.2.pieces_ref
  78.7 1.7 %sum_pieces.1 = f32[8,2,256]{2,1,0:T(2,128)} custom-call(bf16[64,8,512]{2,1,0:T(8,128)(2,1)} %all-to-all-done.2.pieces_ref), custom_call_target="tpu_custom_call" | custom-call | tf_op jit(solution)/shard_map/sum_pieces/pallas_call | solution.py:361
  (14 shorter events, 0.1 us)
Async XLA Ops:
  0.6 2.2 %copy-start.12 = (bf16[8,2,256]{2,1,0:T(2,128)(2,1)S(1)}, bf16[8,2,256]{2,1,0:T(2,128)(2,1)}, u32[]{:S(2)}) copy-start(bf16[8,2,256]{2,1,0:T(2,128)(2,1)} %param.11) | copy-start | bytes 24580
  1.6 17.9 %collective-permute-start = (bf16[128,512]{1,0:T(8,128)(2,1)S(1)}, bf16[128,512]{1,0:T(8,128)(2,1)S(1)}, u32[]{:S(2)}, u32[]{:S(2)}) collective-permute-start(bf16[128,512]{1,0:T(8,128)(2,1)S(1)} %bitcast.19), channel_id=1, source_target_pairs={{0,4},{4,0},{1,5},{5,1},{2,6},{6,2},{3,7},{7,3},{8,12},{12,8},{9,1... | collective-permute-start | bytes 393224 | tf_op jit(solution)/shard_map/ppermute | solution.py:249
  20.4 17.3 %copy-start.2 = (bf16[1,128,16,128]{3,2,1,0:T(8,128)(2,1)S(1)}, bf16[1,128,16,128]{3,2,1,0:T(8,128)(2,1)}, u32[]{:S(2)}) copy-start(bf16[1,128,16,128]{3,2,1,0:T(8,128)(2,1)} %param.15) | copy-start | bytes 1572868
  20.4 13.6 %all-to-all-start.1 = ((bf16[8,64,512]{2,1,0:T(8,128)(2,1)}), bf16[8,64,512]{2,1,0:T(8,128)(2,1)S(1)}, u32[]{:S(2)}, u32[]{:S(2)}) async-start(bf16[8,64,512]{2,1,0:T(8,128)(2,1)} %broadcast_in_dim.23), calls=%async_computation.1 | async-start | bytes 1048576 | tf_op jit(solution)/shard_map/all_to_all | solution.py:260
  25.2 12.5 %copy-start.1 = (bf16[1,128,16,128]{3,2,1,0:T(8,128)(2,1)S(1)}, bf16[1,128,16,128]{3,2,1,0:T(8,128)(2,1)}, u32[]{:S(2)}) copy-start(bf16[1,128,16,128]{3,2,1,0:T(8,128)(2,1)} %param.10) | copy-start | bytes 1572868
  25.2 12.5 %copy-start.11 = (f32[1,16]{1,0:T(1,128)S(1)}, f32[1,16]{1,0:T(1,128)}, u32[]{:S(2)}) copy-start(f32[1,16]{1,0:T(1,128)} %gate_ref.1) | copy-start | bytes 196
  25.3 7.7 %collective-permute-start.1 = (bf16[256,512]{1,0:T(8,128)(2,1)S(1)}, bf16[256,512]{1,0:T(8,128)(2,1)S(1)}, u32[]{:S(2)}, u32[]{:S(2)}) collective-permute-start(bf16[256,512]{1,0:T(8,128)(2,1)S(1)} %pair.1.refs_0_), channel_id=1, source_target_pairs={{0,8},{8,16},{16,24},{24,32},{32,40},{40,48},{48,56},{56,0},{1,9},... | collective-permute-start | bytes 786440 | tf_op jit(solution)/shard_map/ppermute | solution.py:263
  25.9 7.0 %collective-permute-start.2 = (bf16[256,512]{1,0:T(8,128)(2,1)S(1)}, bf16[256,512]{1,0:T(8,128)(2,1)S(1)}, u32[]{:S(2)}, u32[]{:S(2)}) collective-permute-start(bf16[256,512]{1,0:T(8,128)(2,1)S(1)} %pair.1.refs_0_), channel_id=1, source_target_pairs={{0,56},{8,0},{16,8},{24,16},{32,24},{40,32},{48,40},{56,48},{1,57}... | collective-permute-start | bytes 786440 | tf_op jit(solution)/shard_map/ppermute | solution.py:263
  28.6 4.4 %collective-permute-start.3 = (bf16[256,512]{1,0:T(8,128)(2,1)S(1)}, bf16[256,512]{1,0:T(8,128)(2,1)S(1)}, u32[]{:S(2)}, u32[]{:S(2)}) collective-permute-start(bf16[256,512]{1,0:T(8,128)(2,1)S(1)} %pair.1.refs_0_), channel_id=1, source_target_pairs={{0,2},{2,0},{1,3},{3,1},{4,6},{6,4},{5,7},{7,5},{8,10},{10,8},{9,1... | collective-permute-start | bytes 786440 | tf_op jit(solution)/shard_map/ppermute | solution.py:264
  32.9 0.7 copy-start.3
  33.9 3.8 %collective-permute-start.4 = (bf16[512,512]{1,0:T(8,128)(2,1)S(1)}, bf16[512,512]{1,0:T(8,128)(2,1)S(1)}, u32[]{:S(2)}, u32[]{:S(2)}) collective-permute-start(bf16[512,512]{1,0:T(8,128)(2,1)S(1)} %bitcast.17), channel_id=1, source_target_pairs={{0,2},{2,0},{1,3},{3,1},{4,6},{6,4},{5,7},{7,5},{8,10},{10,8},{9,1... | collective-permute-start | bytes 1572872 | tf_op jit(solution)/shard_map/ppermute | solution.py:267
  33.9 13.0 %collective-permute-start.5 = (bf16[256,512]{1,0:T(8,128)(2,1)S(1)}, bf16[256,512]{1,0:T(8,128)(2,1)S(1)}, u32[]{:S(2)}, u32[]{:S(2)}) collective-permute-start(bf16[256,512]{1,0:T(8,128)(2,1)S(1)} %collective-permute-done.1.refs_1_), channel_id=1, source_target_pairs={{0,2},{2,0},{1,3},{3,1},{4,6},{6,4},{5,7},{7,5},{8,10},{10,8},{9,1... | collective-permute-start | bytes 786440 | tf_op jit(solution)/shard_map/ppermute | solution.py:269
  34.4 12.5 %collective-permute-start.7 = (bf16[256,512]{1,0:T(8,128)(2,1)S(1)}, bf16[256,512]{1,0:T(8,128)(2,1)}, u32[]{:S(2)}, u32[]{:S(2)}) collective-permute-start(bf16[256,512]{1,0:T(8,128)(2,1)S(1)} %collective-permute-done.1.refs_1_), channel_id=1, source_target_pairs={{0,8},{8,16},{16,24},{24,32},{32,40},{40,48},{48,56},{56,0},{1,9},... | collective-permute-start | bytes 786440 | tf_op jit(solution)/shard_map/ppermute | solution.py:268
  35.0 11.9 %collective-permute-start.6 = (bf16[256,512]{1,0:T(8,128)(2,1)S(1)}, bf16[256,512]{1,0:T(8,128)(2,1)S(1)}, u32[]{:S(2)}, u32[]{:S(2)}) collective-permute-start(bf16[256,512]{1,0:T(8,128)(2,1)S(1)} %collective-permute-done.2.refs_2_), channel_id=1, source_target_pairs={{0,2},{2,0},{1,3},{3,1},{4,6},{6,4},{5,7},{7,5},{8,10},{10,8},{9,1... | collective-permute-start | bytes 786440 | tf_op jit(solution)/shard_map/ppermute | solution.py:269
  35.0 11.9 %collective-permute-start.8 = (bf16[256,512]{1,0:T(8,128)(2,1)S(1)}, bf16[256,512]{1,0:T(8,128)(2,1)}, u32[]{:S(2)}, u32[]{:S(2)}) collective-permute-start(bf16[256,512]{1,0:T(8,128)(2,1)S(1)} %collective-permute-done.2.refs_2_), channel_id=1, source_target_pairs={{0,56},{8,0},{16,8},{24,16},{32,24},{40,32},{48,40},{56,48},{1,57}... | collective-permute-start | bytes 786440 | tf_op jit(solution)/shard_map/ppermute | solution.py:268
  37.7 0.7 copy-start.9
  37.7 0.7 copy-start.10
  46.9 4.9 %copy-start.5 = (bf16[256,512]{1,0:T(8,128)(2,1)}, bf16[256,512]{1,0:T(8,128)(2,1)S(1)}, u32[]{:S(2)}) copy-start(bf16[256,512]{1,0:T(8,128)(2,1)S(1)} %collective-permute-done.5.refs_8_) | copy-start | bytes 786436
  46.9 4.8 %copy-start.7 = (bf16[256,512]{1,0:T(8,128)(2,1)}, bf16[256,512]{1,0:T(8,128)(2,1)S(1)}, u32[]{:S(2)}) copy-start(bf16[256,512]{1,0:T(8,128)(2,1)S(1)} %collective-permute-done.6.refs_9_) | copy-start | bytes 786436
  46.9 3.8 %collective-permute-start.9 = (bf16[512,512]{1,0:T(8,128)(2,1)S(1)}, bf16[512,512]{1,0:T(8,128)(2,1)S(1)}, u32[]{:S(2)}, u32[]{:S(2)}) collective-permute-start(bf16[512,512]{1,0:T(8,128)(2,1)S(1)} %get-tuple-element.36), channel_id=1, source_target_pairs={{0,2},{2,0},{1,3},{3,1},{4,6},{6,4},{5,7},{7,5},{8,10},{10,8},{9,1... | collective-permute-start | bytes 1572872 | tf_op jit(solution)/shard_map/ppermute | solution.py:293
  47.2 4.5 %collective-permute-start.10 = (bf16[256,512]{1,0:T(8,128)(2,1)}, bf16[256,512]{1,0:T(8,128)(2,1)S(1)}, u32[]{:S(2)}, u32[]{:S(2)}) collective-permute-start(bf16[256,512]{1,0:T(8,128)(2,1)} %collective-permute-done.7.refs_3_), channel_id=1, source_target_pairs={{0,2},{2,0},{1,3},{3,1},{4,6},{6,4},{5,7},{7,5},{8,10},{10,8},{9,1... | collective-permute-start | bytes 786440 | tf_op jit(solution)/shard_map/ppermute | solution.py:295
  47.5 11.5 %collective-permute-start.12 = (bf16[256,512]{1,0:T(8,128)(2,1)}, bf16[256,512]{1,0:T(8,128)(2,1)S(1)}, u32[]{:S(2)}, u32[]{:S(2)}) collective-permute-start(bf16[256,512]{1,0:T(8,128)(2,1)} %collective-permute-done.7.refs_3_), channel_id=1, source_target_pairs={{0,8},{8,16},{16,24},{24,32},{32,40},{40,48},{48,56},{56,0},{1,9},... | collective-permute-start | bytes 786440 | tf_op jit(solution)/shard_map/ppermute | solution.py:294
  47.5 4.2 %collective-permute-start.11 = (bf16[256,512]{1,0:T(8,128)(2,1)}, bf16[256,512]{1,0:T(8,128)(2,1)S(1)}, u32[]{:S(2)}, u32[]{:S(2)}) collective-permute-start(bf16[256,512]{1,0:T(8,128)(2,1)} %collective-permute-done.8.refs_4_), channel_id=1, source_target_pairs={{0,2},{2,0},{1,3},{3,1},{4,6},{6,4},{5,7},{7,5},{8,10},{10,8},{9,1... | collective-permute-start | bytes 786440 | tf_op jit(solution)/shard_map/ppermute | solution.py:295
  47.7 11.4 %collective-permute-start.13 = (bf16[256,512]{1,0:T(8,128)(2,1)}, bf16[256,512]{1,0:T(8,128)(2,1)S(1)}, u32[]{:S(2)}, u32[]{:S(2)}) collective-permute-start(bf16[256,512]{1,0:T(8,128)(2,1)} %collective-permute-done.8.refs_4_), channel_id=1, source_target_pairs={{0,56},{8,0},{16,8},{24,16},{32,24},{40,32},{48,40},{56,48},{1,57}... | collective-permute-start | bytes 786440 | tf_op jit(solution)/shard_map/ppermute | solution.py:294
  51.7 9.5 %copy-start.6 = (bf16[256,512]{1,0:T(8,128)(2,1)S(1)}, bf16[256,512]{1,0:T(8,128)(2,1)}, u32[]{:S(2)}) copy-start(bf16[256,512]{1,0:T(8,128)(2,1)} %copy-done.5) | copy-start | bytes 786436
  51.8 9.5 %copy-start.8 = (bf16[256,512]{1,0:T(8,128)(2,1)S(1)}, bf16[256,512]{1,0:T(8,128)(2,1)}, u32[]{:S(2)}) copy-start(bf16[256,512]{1,0:T(8,128)(2,1)} %copy-done.7) | copy-start | bytes 786436
  51.8 26.9 %all-to-all-start.2 = ((bf16[64,8,512]{2,1,0:T(8,128)(2,1)}), bf16[64,8,512]{2,1,0:T(8,128)(2,1)}, u32[]{:S(2)}, u32[]{:S(2)}) async-start(bf16[64,8,512]{2,1,0:T(8,128)(2,1)} %fusion), calls=%async_computation.2 | async-start | bytes 1048576 | tf_op jit(solution)/shard_map/all_to_all | solution.py:298
  59.0 2.3 %copy-start = (bf16[1,128,16,128]{3,2,1,0:T(8,128)(2,1)S(1)}, bf16[1,128,16,128]{3,2,1,0:T(8,128)(2,1)}, u32[]{:S(2)}) copy-start(bf16[1,128,16,128]{3,2,1,0:T(8,128)(2,1)} %param.8) | copy-start | bytes 1572868
  59.0 2.3 %copy-start.4 = (bf16[256,512]{1,0:T(8,128)(2,1)S(1)}, bf16[256,512]{1,0:T(8,128)(2,1)}, u32[]{:S(2)}) copy-start(bf16[256,512]{1,0:T(8,128)(2,1)} %copy-done.3) | copy-start | bytes 786436
  59.1 2.2 %collective-permute-start.15 = (bf16[256,512]{1,0:T(8,128)(2,1)S(1)}, bf16[256,512]{1,0:T(8,128)(2,1)S(1)}, u32[]{:S(2)}, u32[]{:S(2)}) collective-permute-start(bf16[256,512]{1,0:T(8,128)(2,1)S(1)} %collective-permute-done.12.first_ref.refs_5_), channel_id=1, source_target_pairs={{0,2},{2,0},{1,3},{3,1},{4,6},{6,4},{5,7},{7,5},{8,10},{10,8},{9,1... | collective-permute-start | bytes 786440 | tf_op jit(solution)/shard_map/ppermute | solution.py:333
  59.2 2.1 %collective-permute-start.16 = (bf16[256,512]{1,0:T(8,128)(2,1)S(1)}, bf16[256,512]{1,0:T(8,128)(2,1)S(1)}, u32[]{:S(2)}, u32[]{:S(2)}) collective-permute-start(bf16[256,512]{1,0:T(8,128)(2,1)S(1)} %collective-permute-done.13.second_ref.refs_6_), channel_id=1, source_target_pairs={{0,2},{2,0},{1,3},{3,1},{4,6},{6,4},{5,7},{7,5},{8,10},{10,8},{9,1... | collective-permute-start | bytes 786440 | tf_op jit(solution)/shard_map/ppermute | solution.py:333
  59.7 16.2 %collective-permute-start.14 = (bf16[256,512]{1,0:T(8,128)(2,1)S(1)}, bf16[256,512]{1,0:T(8,128)(2,1)S(1)}, u32[]{:S(2)}, u32[]{:S(2)}) collective-permute-start(bf16[256,512]{1,0:T(8,128)(2,1)S(1)} %pick.1), channel_id=1, source_target_pairs={{0,8},{2,58},{8,16},{10,2},{16,24},{18,10},{24,32},{26,18},{32,40}... | collective-permute-start | bytes 786440 | tf_op jit(solution)/shard_map/ppermute | solution.py:332
  75.9 1.5 %collective-permute-start.17 = (bf16[256,512]{1,0:T(8,128)(2,1)S(1)}, bf16[256,512]{1,0:T(8,128)(2,1)S(1)}, u32[]{:S(2)}, u32[]{:S(2)}) collective-permute-start(bf16[256,512]{1,0:T(8,128)(2,1)S(1)} %collective-permute-done.14.refs_0_), channel_id=1, source_target_pairs={{0,2},{2,0},{1,3},{3,1},{4,6},{6,4},{5,7},{7,5},{8,10},{10,8},{9,1... | collective-permute-start | bytes 786440 | tf_op jit(solution)/shard_map/ppermute | solution.py:348

commit v3 on v2

--- a/solution.py
+++ b/solution.py
@@ -30,45 +30,39 @@
     return jnp.transpose(a.astype(F32), (1, 0)).astype(a.dtype)
 
 
-def cross_kernel(
-    image_ref,
-    mask_ref,
-    cq_ref,
-    cot_ref,
-    gate_ref,
-    va_ref,
-    vb_ref,
-    out_ref,
-    gq_ref,
-    ga_ref,
-    gb_ref,
-):
-    h = pl.program_id(0)
+def info_kernel(image_ref, mask_ref, gate_ref, bias_ref, gate_out):
     core = lax.axis_index("c")
-    half = va_ref.shape[0]
-    count = 2 * half
-    rows = cq_ref.shape[0] * 8
+    count = bias_ref.shape[1]
+    half = count // 2
     lane = lax.broadcasted_iota(jnp.int32, (1, count), 1)
     which = jnp.where(lane < half, core, 1 - core)
     part = lane % half // 8
     token = (((part // 16 * 8 + part % 8) * 2 + part // 8 % 2) * 2 + which) * 8 + lane % 8
-    live = []
     for rb in range(2):
         on = jnp.zeros((1, count), jnp.int32) + mask_ref[rb, 0]
         bound = 0
         for k in range(IMAGES - 1):
             bound = bound + image_ref[k]
             on = jnp.where(token >= bound, mask_ref[rb, k + 1], on)
-        live.append(jnp.broadcast_to(jnp.where(on == 1, 0.0, NEG), (rows // 2, count)))
-    bias = jnp.concatenate(live, axis=0)
-
+        bias_ref[rb : rb + 1, :] = jnp.where(on == 1, 0.0, NEG)
+    head = lax.broadcasted_iota(jnp.int32, (16, 16), 0)
+    chosen = lax.broadcasted_iota(jnp.int32, (16, 16), 1) == head
+    gates = jnp.where(chosen, jnp.broadcast_to(gate_ref[...], (16, 16)), 0.0)
+    gate_out[...] = jnp.tanh(jnp.broadcast_to(jnp.sum(gates, axis=1, keepdims=True), (16, HD)))
+
+
+def cross_kernel(
+    bias_ref, cq_ref, cot_ref, gate_ref, va_ref, vb_ref, out_ref, gq_ref, ga_ref, gb_ref
+):
+    half = va_ref.shape[0]
+    count = 2 * half
+    rows = cq_ref.shape[0] * 8
+    bias = jnp.concatenate(
+        [jnp.broadcast_to(bias_ref[rb : rb + 1, :], (rows // 2, count)) for rb in range(2)], axis=0
+    )
+    gate = gate_ref[...]
     keys = jnp.concatenate([va_ref[:, :HD], vb_ref[:, :HD]], axis=0)
     values = jnp.concatenate([va_ref[:, HD:], vb_ref[:, HD:]], axis=0)
-    head = lax.broadcasted_iota(jnp.int32, (8, 16), 0) + h * 8
-    chosen = lax.broadcasted_iota(jnp.int32, (8, 16), 1) == head
-    gates = jnp.where(chosen, jnp.broadcast_to(gate_ref[...], (8, 16)), 0.0)
-    gate = jnp.tanh(jnp.broadcast_to(jnp.sum(gates, axis=1, keepdims=True), (8, HD)))
-
     q = cq_ref[...].reshape(rows, HD)
     go = (cot_ref[...].astype(F32) * gate[None]).astype(BF16).reshape(rows, HD)
     s = nt(q, keys) * SCALE2 + bias
@@ -263,12 +257,23 @@
     up1, down1 = lax.ppermute(pair, "z", up), lax.ppermute(pair, "z", down)
     pair_c = lax.ppermute(pair, "c", swap)
 
-    va, up1, down1, pair_c = tie((va, up1, down1, pair_c))
+    smem = pl.BlockSpec(memory_space=pltpu.SMEM)
+    bias, gate = pl.pallas_call(
+        info_kernel,
+        out_shape=(
+            jax.ShapeDtypeStruct((2, 2 * tokens), F32),
+            jax.ShapeDtypeStruct((16, HD), F32),
+        ),
+        in_specs=[smem, smem, spec()],
+        out_specs=[spec()] * 2,
+        compiler_params=pltpu.CompilerParams(vmem_limit_bytes=4 << 20),
+        name="mask_and_gate",
+    )(image_tokens, cross_mask, cross_gate)
+    va, up1, down1, pair_c, bias, gate = tie((va, up1, down1, pair_c, bias, gate))
     vb = lax.ppermute(va, "c", swap)
     up2, down2 = lax.ppermute(up1, "z", up), lax.ppermute(down1, "z", down)
     up1c, down1c = lax.ppermute(up1, "c", swap), lax.ppermute(down1, "c", swap)
 
-    smem = pl.BlockSpec(memory_space=pltpu.SMEM)
     by_head = pl.BlockSpec((128, 8, HD), lambda h: (0, h, 0))
     by_lane = pl.BlockSpec((tokens, 2 * HD), lambda h: (0, h))
     cross, grad_q, grad_own, grad_other = pl.pallas_call(
@@ -280,14 +285,21 @@
             jax.ShapeDtypeStruct((tokens, 4 * HD), F32),
             jax.ShapeDtypeStruct((tokens, 4 * HD), BF16),
         ),
-        in_specs=[smem, smem, by_head, by_head, spec(), by_lane, by_lane],
+        in_specs=[
+            spec(),
+            by_head,
+            by_head,
+            pl.BlockSpec((8, HD), lambda h: (h, 0)),
+            by_lane,
+            by_lane,
+        ],
         out_specs=[by_head, by_head, by_lane, by_lane],
         compiler_params=pltpu.CompilerParams(vmem_limit_bytes=40 << 20),
         cost_estimate=pl.CostEstimate(
             flops=6 * 2 * 2 * 1024 * 1024 * 128, bytes_accessed=6 << 20, transcendentals=2 << 20
         ),
         name="cross_attention",
-    )(image_tokens, cross_mask, cross_q[0], out_cotangent[0], cross_gate, va, vb)
+    )(bias, cross_q[0], out_cotangent[0], gate, va, vb)
 
     grad_other, up1c, down1c, up2, down2 = tie((grad_other, up1c, down1c, up2, down2))
     received = lax.ppermute(grad_other, "c", swap)

time: 82 us -> 80.9 us (0.987)
  no operation moved by 1% of the time
where the time goes in v3:
time: 80.9 us; the launch traced here: 79.4 us
  starting transfers between devices  26.5 us (33%)
  waiting for transfers between devices  17.3 us (21%)
  blocking collectives  16.6 us (21%)
  Pallas kernels  14.6 us (18%)
  local copies, waits for them, and re-layouts  2.54 us (3%)
  other arithmetic  0.97 us (1%)
  between operations  0.88 us (1%)
    all_to_all x1, blocking collectives, shards(): column = lax.all_to_all(image, 'z', 0, 0, tiled=True).reshape(1, 64, 4 * HD)  16.6 us
    ppermute x1, waiting for transfers between devices, shards(): last = lax.ppermute(split, ('z', 'c'), halves)  11.8 us
    pallas_call x1, Pallas kernels, shards(): pl.pallas_call(cross_kernel, grid=(2,), out_shape=(jax.ShapeDtypeStruct((...  8.15 us
    all_to_all x1, starting transfers between devices, shards(): pieces = lax.all_to_all(partial, ring, 0, 0, tiled=True)  7.28 us
    all_to_all x1, starting transfers between devices, shards(): lax.all_to_all(jnp.broadcast_to(column, (8, 64, 4 * HD)), ('y', 'x'), 0,...  4.87 us
    ppermute x2, waiting for transfers between devices, shards(): up1, down1 = (lax.ppermute(pair, 'z', up), lax.ppermute(pair, 'z', down))  3.69 us
    ppermute x2, starting transfers between devices, shards(): up1, down1 = (lax.ppermute(pair, 'z', up), lax.ppermute(pair, 'z', down))  3.31 us
    ppermute x2, starting transfers between devices, shards(): up2, down2 = (lax.ppermute(up1, 'z', up), lax.ppermute(down1, 'z', down))  3.24 us
  transfers between devices with their start and end apart: 20, of which 4 were waited for; matrix products, arithmetic and copies ran while one was open for 1% of the time, Pallas kernels for 16%

profile of v3, /device:TPU:4, one launch (start us, length us, event | category | flops | bytes accessed | tf_op | source)
XLA Modules:
  0.0 79.4 jit_solution(14604459268681753036)
XLA Ops:
  0.6 0.0 copy-start.12
  0.6 0.9 %copy.12 = bf16[16,8,2,256]{3,1,2,0:T(8,128)(2,1)S(1)} copy(bf16[16,8,2,256]{3,2,1,0:T(2,128)(2,1)} %bitcast.25) | data formatting | bytes 262144
  1.6 1.3 %collective-permute-start = (bf16[128,512]{1,0:T(8,128)(2,1)S(1)}, bf16[128,512]{1,0:T(8,128)(2,1)S(1)}, u32[]{:S(2)}, u32[]{:S(2)}) collective-permute-start(bf16[128,512]{1,0:T(8,128)(2,1)S(1)} %bitcast.19), channel_id=1, source_target_pairs={{0,4},{4,0},{1,5},{5,1},{2,6},{6,2},{3,7},{7,3},{8,12},{12,8},{9,1... | collective-permute-start | bytes 393224 | tf_op jit(solution)/shard_map/ppermute | solution.py:243
  2.9 0.0 copy-done.12
  2.9 16.6 %all_to_all.15 = bf16[8,8,512]{2,1,0:T(8,128)(2,1)S(1)} all-to-all(bf16[8,8,512]{2,1,0:T(8,128)(2,1)S(1)} %broadcast_in_dim.21), channel_id=1, replica_groups=mesh['y'=4,'z'=8,'x'=2,'c'=2,'t'=2] {'z'}, dimensions={0} | all-to-all | bytes 131072 | tf_op jit(solution)/shard_map/all_to_all | solution.py:244
  19.5 0.0 collective-permute-done.other_ref
  19.5 0.8 %broadcast_in_dim.23 = bf16[8,64,512]{2,1,0:T(8,128)(2,1)} broadcast(bf16[64,512]{1,0:T(8,128)(2,1)S(1)} %bitcast.24), dimensions={1,2} | broadcast | bytes 589824 | tf_op jit(solution)/shard_map/broadcast_in_dim | solution.py:255
  20.4 4.9 %all-to-all-start.1 = ((bf16[8,64,512]{2,1,0:T(8,128)(2,1)}), bf16[8,64,512]{2,1,0:T(8,128)(2,1)S(1)}, u32[]{:S(2)}, u32[]{:S(2)}) async-start(bf16[8,64,512]{2,1,0:T(8,128)(2,1)} %broadcast_in_dim.23), calls=%async_computation.1 | async-start | bytes 1048576 | tf_op jit(solution)/shard_map/all_to_all | solution.py:254
  25.2 0.0 copy-start.2
  25.2 0.0 copy-start.3
  25.2 0.0 copy-start.4
  25.3 0.6 collective-permute-start.1
  25.9 2.7 %collective-permute-start.2 = (bf16[256,512]{1,0:T(8,128)(2,1)S(1)}, bf16[256,512]{1,0:T(8,128)(2,1)S(1)}, u32[]{:S(2)}, u32[]{:S(2)}) collective-permute-start(bf16[256,512]{1,0:T(8,128)(2,1)S(1)} %pair.1.refs_0_), channel_id=1, source_target_pairs={{0,56},{8,0},{16,8},{24,16},{32,24},{40,32},{48,40},{56,48},{1,57}... | collective-permute-start | bytes 786440 | tf_op jit(solution)/shard_map/ppermute | solution.py:257
  28.6 0.0 collective-permute-start.3
  28.6 0.0 copy-done.1
  28.6 0.0 copy-done.2
  28.6 0.0 copy-done.3
  28.6 0.6 mask_and_gate.1
  29.3 3.7 %collective-permute-done.1.refs_1_ = bf16[256,512]{1,0:T(8,128)(2,1)S(1)} collective-permute-done((bf16[256,512]{1,0:T(8,128)(2,1)S(1)}, bf16[256,512]{1,0:T(8,128)(2,1)S(1)}, u32[]{:S(2)}, u32[]{:S(2)}) %collective-permute-start.1) | collective-permute-done | bytes 262176 | tf_op jit(solution)/shard_map/ppermute | solution.py:257
  33.0 0.0 collective-permute-done.2.refs_2_
  33.0 0.0 collective-permute-done.3.refs_7_
  33.0 0.7 copy-done.6
  33.7 0.2 all-to-all-done.1
  33.9 0.0 collective-permute-start.4
  33.9 0.5 collective-permute-start.5
  34.4 0.6 collective-permute-start.7
  35.0 0.0 collective-permute-start.6
  35.0 2.7 %collective-permute-start.8 = (bf16[256,512]{1,0:T(8,128)(2,1)S(1)}, bf16[256,512]{1,0:T(8,128)(2,1)}, u32[]{:S(2)}, u32[]{:S(2)}) collective-permute-start(bf16[256,512]{1,0:T(8,128)(2,1)S(1)} %collective-permute-done.2.refs_2_), channel_id=1, source_target_pairs={{0,56},{8,0},{16,8},{24,16},{32,24},{40,32},{48,40},{56,48},{1,57}... | collective-permute-start | bytes 786440 | tf_op jit(solution)/shard_map/ppermute | solution.py:274
  37.7 0.0 collective-permute-done.4.vb_ref
  37.7 0.0 copy-done.5
  37.7 0.0 copy-done.4
  37.7 8.2 %cross_attention.1 = (f32[128,16,128]{2,1,0:T(8,128)S(1)}, bf16[128,16,128]{2,1,0:T(8,128)(2,1)}, f32[512,512]{1,0:T(8,128)S(1)}, bf16[512,512]{1,0:T(8,128)(2,1)S(1)}) custom-call(f32[2,1024]{1,0:T(2,128)S(1)} %get-tuple-element.37.bias_ref, bf16[128,16,128]{2,1,0:T(8,128)(2,1)S(1)} %bitcast.21, bf16[128,16,128]{2,1,0:T(8,128)(2,1)S(1)} %bitcast.22, ...), custom_call_target="tpu_custom_call" | custom-call | flops 3221225472 | bytes 6291456 | tf_op jit(solution)/shard_map/cross_attention/pallas_call | solution.py:279
  45.8 0.0 collective-permute-done.5.refs_8_
  45.8 0.0 collective-permute-done.6.refs_9_
  45.8 0.0 copy-start.10
  45.8 0.0 collective-permute-done.7.refs_3_
  45.9 0.0 collective-permute-done.8.refs_4_
  45.9 0.3 collective-permute-start.9
  46.2 0.3 collective-permute-start.10
  46.5 0.0 collective-permute-start.12
  46.5 0.2 collective-permute-start.11
  46.7 3.0 %collective-permute-start.13 = (bf16[256,512]{1,0:T(8,128)(2,1)}, bf16[256,512]{1,0:T(8,128)(2,1)S(1)}, u32[]{:S(2)}, u32[]{:S(2)}) collective-permute-start(bf16[256,512]{1,0:T(8,128)(2,1)} %collective-permute-done.8.refs_4_), channel_id=1, source_target_pairs={{0,56},{8,0},{16,8},{24,16},{32,24},{40,32},{48,40},{56,48},{1,57}... | collective-permute-start | bytes 786440 | tf_op jit(solution)/shard_map/ppermute | solution.py:306
  49.7 0.0 collective-permute-done.9
  49.7 1.0 %fusion = bf16[64,8,512]{2,1,0:T(8,128)(2,1)} fusion(f32[512,512]{1,0:T(8,128)S(1)} %get-tuple-element.40, bf16[512,512]{1,0:T(8,128)(2,1)S(1)} %collective-permute-done.9), kind=kLoop, calls=%fused_computation.1 | loop fusion | flops 786432 | bytes 2097152 | tf_op jit(solution)/shard_map/reshape | solution.py:308
  50.7 0.0 copy-done.8
  50.7 0.0 collective-permute-done.10.refs_10_
  50.7 0.0 collective-permute-done.11.refs_11_
  50.7 0.0 copy-start.9
  50.7 7.3 %all-to-all-start.2 = ((bf16[64,8,512]{2,1,0:T(8,128)(2,1)}), bf16[64,8,512]{2,1,0:T(8,128)(2,1)}, u32[]{:S(2)}, u32[]{:S(2)}) async-start(bf16[64,8,512]{2,1,0:T(8,128)(2,1)} %fusion), calls=%async_computation.2 | async-start | bytes 1048576 | tf_op jit(solution)/shard_map/all_to_all | solution.py:310
  58.0 0.0 copy-start
  58.0 0.0 collective-permute-done.12.first_ref.refs_5_
  58.0 0.1 collective-permute-start.15
  58.1 0.0 collective-permute-done.13.second_ref.refs_6_
  58.2 0.5 collective-permute-start.16
  58.7 1.6 %collective-permute-start.14 = (bf16[256,512]{1,0:T(8,128)(2,1)S(1)}, bf16[256,512]{1,0:T(8,128)(2,1)S(1)}, u32[]{:S(2)}, u32[]{:S(2)}) collective-permute-start(bf16[256,512]{1,0:T(8,128)(2,1)S(1)} %pick.1), channel_id=1, source_target_pairs={{0,8},{2,58},{8,16},{10,2},{16,24},{18,10},{24,32},{26,18},{32,40}... | collective-permute-start | bytes 786440 | tf_op jit(solution)/shard_map/ppermute | solution.py:344
  60.2 0.0 collective-permute-done.15.refs_12_
  60.2 0.0 collective-permute-done.16.refs_13_
  60.3 2.7 %self_near.1 = (f32[2,1024,128]{2,1,0:T(8,128)S(1)}, f32[2,1024,128]{2,1,0:T(8,128)S(1)}) custom-call(bf16[256,512]{1,0:T(8,128)(2,1)S(1)} %pair.1.refs_0_, bf16[256,512]{1,0:T(8,128)(2,1)S(1)} %collective-permute-done.1.refs_1_, bf16[256,512]{1,0:T(8,128)(2,1)S(1)} %collective-permute-done.2.refs_2_, bf16[256,512]{1,0:T(8,128)(2,1)} %collective-permute-done.7.refs_3_, ...), custom_call_target="tpu_custom_call" | custom-call | flops 3758096384 | bytes 6291456 | tf_op jit(solution)/shard_map/self_near/pallas_call | solution.py:348
  63.0 11.8 %collective-permute-done.14.refs_0_ = bf16[256,512]{1,0:T(8,128)(2,1)S(1)} collective-permute-done((bf16[256,512]{1,0:T(8,128)(2,1)S(1)}, bf16[256,512]{1,0:T(8,128)(2,1)S(1)}, u32[]{:S(2)}, u32[]{:S(2)}) %collective-permute-start.14) | collective-permute-done | bytes 262176 | tf_op jit(solution)/shard_map/ppermute | solution.py:344
  74.8 0.0 collective-permute-start.17
  74.8 1.5 %collective-permute-done.17.refs_1_ = bf16[256,512]{1,0:T(8,128)(2,1)S(1)} collective-permute-done((bf16[256,512]{1,0:T(8,128)(2,1)S(1)}, bf16[256,512]{1,0:T(8,128)(2,1)S(1)}, u32[]{:S(2)}, u32[]{:S(2)}) %collective-permute-start.17) | collective-permute-done | bytes 262176 | tf_op jit(solution)/shard_map/ppermute | solution.py:360
  76.4 1.3 %self_far.1 = bf16[128,16,128]{2,1,0:T(8,128)(2,1)} custom-call(bf16[256,512]{1,0:T(8,128)(2,1)S(1)} %collective-permute-done.14.refs_0_, bf16[256,512]{1,0:T(8,128)(2,1)S(1)} %collective-permute-done.17.refs_1_, bf16[128,16,128]{2,1,0:T(8,128)(2,1)S(1)} %bitcast.16, f32[2,1024,128]{2,1,0:T(8,128)S(1)} %get-tuple-element.55.refs_3_, ...), custom_call_target="tpu_custom_call" | custom-call | flops 536870912 | bytes 6291456 | tf_op jit(solution)/shard_map/self_far/pallas_call | solution.py:361
  77.7 0.0 all-to-all-done.2.pieces_ref
  77.7 1.7 %sum_pieces.1 = f32[8,2,256]{2,1,0:T(2,128)} custom-call(bf16[64,8,512]{2,1,0:T(8,128)(2,1)} %all-to-all-done.2.pieces_ref), custom_call_target="tpu_custom_call" | custom-call | tf_op jit(solution)/shard_map/sum_pieces/pallas_call | solution.py:373
  (15 shorter events, 0.1 us)
Async XLA Ops:
  0.6 2.2 %copy-start.12 = (bf16[8,2,256]{2,1,0:T(2,128)(2,1)S(1)}, bf16[8,2,256]{2,1,0:T(2,128)(2,1)}, u32[]{:S(2)}) copy-start(bf16[8,2,256]{2,1,0:T(2,128)(2,1)} %param.11) | copy-start | bytes 24580
  1.6 17.9 %collective-permute-start = (bf16[128,512]{1,0:T(8,128)(2,1)S(1)}, bf16[128,512]{1,0:T(8,128)(2,1)S(1)}, u32[]{:S(2)}, u32[]{:S(2)}) collective-permute-start(bf16[128,512]{1,0:T(8,128)(2,1)S(1)} %bitcast.19), channel_id=1, source_target_pairs={{0,4},{4,0},{1,5},{5,1},{2,6},{6,2},{3,7},{7,3},{8,12},{12,8},{9,1... | collective-permute-start | bytes 393224 | tf_op jit(solution)/shard_map/ppermute | solution.py:243
  20.4 17.3 %copy-start.5 = (bf16[1,128,16,128]{3,2,1,0:T(8,128)(2,1)S(1)}, bf16[1,128,16,128]{3,2,1,0:T(8,128)(2,1)}, u32[]{:S(2)}) copy-start(bf16[1,128,16,128]{3,2,1,0:T(8,128)(2,1)} %param.15) | copy-start | bytes 1572868
  20.4 13.6 %all-to-all-start.1 = ((bf16[8,64,512]{2,1,0:T(8,128)(2,1)}), bf16[8,64,512]{2,1,0:T(8,128)(2,1)S(1)}, u32[]{:S(2)}, u32[]{:S(2)}) async-start(bf16[8,64,512]{2,1,0:T(8,128)(2,1)} %broadcast_in_dim.23), calls=%async_computation.1 | async-start | bytes 1048576 | tf_op jit(solution)/shard_map/all_to_all | solution.py:254
  25.2 3.4 %copy-start.1 = (s32[2,4]{1,0:T(2,128)S(1)}, s32[2,4]{1,0:T(2,128)}, u32[]{:S(2)}) copy-start(s32[2,4]{1,0:T(2,128)} %mask_ref.1) | copy-start | bytes 100
  25.2 3.4 %copy-start.2 = (s32[4]{0:T(128)S(1)}, s32[4]{0:T(128)}, u32[]{:S(2)}) copy-start(s32[4]{0:T(128)} %image_ref.1) | copy-start | bytes 52
  25.2 3.4 %copy-start.3 = (f32[1,16]{1,0:T(1,128)S(1)}, f32[1,16]{1,0:T(1,128)}, u32[]{:S(2)}) copy-start(f32[1,16]{1,0:T(1,128)} %gate_ref.1) | copy-start | bytes 196
  25.2 12.4 %copy-start.4 = (bf16[1,128,16,128]{3,2,1,0:T(8,128)(2,1)S(1)}, bf16[1,128,16,128]{3,2,1,0:T(8,128)(2,1)}, u32[]{:S(2)}) copy-start(bf16[1,128,16,128]{3,2,1,0:T(8,128)(2,1)} %param.10) | copy-start | bytes 1572868
  25.3 7.7 %collective-permute-start.1 = (bf16[256,512]{1,0:T(8,128)(2,1)S(1)}, bf16[256,512]{1,0:T(8,128)(2,1)S(1)}, u32[]{:S(2)}, u32[]{:S(2)}) collective-permute-start(bf16[256,512]{1,0:T(8,128)(2,1)S(1)} %pair.1.refs_0_), channel_id=1, source_target_pairs={{0,8},{8,16},{16,24},{24,32},{32,40},{40,48},{48,56},{56,0},{1,9},... | collective-permute-start | bytes 786440 | tf_op jit(solution)/shard_map/ppermute | solution.py:257
  25.9 7.0 %collective-permute-start.2 = (bf16[256,512]{1,0:T(8,128)(2,1)S(1)}, bf16[256,512]{1,0:T(8,128)(2,1)S(1)}, u32[]{:S(2)}, u32[]{:S(2)}) collective-permute-start(bf16[256,512]{1,0:T(8,128)(2,1)S(1)} %pair.1.refs_0_), channel_id=1, source_target_pairs={{0,56},{8,0},{16,8},{24,16},{32,24},{40,32},{48,40},{56,48},{1,57}... | collective-permute-start | bytes 786440 | tf_op jit(solution)/shard_map/ppermute | solution.py:257
  28.6 4.4 %collective-permute-start.3 = (bf16[256,512]{1,0:T(8,128)(2,1)S(1)}, bf16[256,512]{1,0:T(8,128)(2,1)S(1)}, u32[]{:S(2)}, u32[]{:S(2)}) collective-permute-start(bf16[256,512]{1,0:T(8,128)(2,1)S(1)} %pair.1.refs_0_), channel_id=1, source_target_pairs={{0,2},{2,0},{1,3},{3,1},{4,6},{6,4},{5,7},{7,5},{8,10},{10,8},{9,1... | collective-permute-start | bytes 786440 | tf_op jit(solution)/shard_map/ppermute | solution.py:258
  33.0 0.7 copy-start.6
  33.9 3.8 %collective-permute-start.4 = (bf16[512,512]{1,0:T(8,128)(2,1)S(1)}, bf16[512,512]{1,0:T(8,128)(2,1)S(1)}, u32[]{:S(2)}, u32[]{:S(2)}) collective-permute-start(bf16[512,512]{1,0:T(8,128)(2,1)S(1)} %bitcast.17), channel_id=1, source_target_pairs={{0,2},{2,0},{1,3},{3,1},{4,6},{6,4},{5,7},{7,5},{8,10},{10,8},{9,1... | collective-permute-start | bytes 1572872 | tf_op jit(solution)/shard_map/ppermute | solution.py:273
  33.9 11.9 %collective-permute-start.5 = (bf16[256,512]{1,0:T(8,128)(2,1)S(1)}, bf16[256,512]{1,0:T(8,128)(2,1)S(1)}, u32[]{:S(2)}, u32[]{:S(2)}) collective-permute-start(bf16[256,512]{1,0:T(8,128)(2,1)S(1)} %collective-permute-done.1.refs_1_), channel_id=1, source_target_pairs={{0,2},{2,0},{1,3},{3,1},{4,6},{6,4},{5,7},{7,5},{8,10},{10,8},{9,1... | collective-permute-start | bytes 786440 | tf_op jit(solution)/shard_map/ppermute | solution.py:275
  34.4 11.4 %collective-permute-start.7 = (bf16[256,512]{1,0:T(8,128)(2,1)S(1)}, bf16[256,512]{1,0:T(8,128)(2,1)}, u32[]{:S(2)}, u32[]{:S(2)}) collective-permute-start(bf16[256,512]{1,0:T(8,128)(2,1)S(1)} %collective-permute-done.1.refs_1_), channel_id=1, source_target_pairs={{0,8},{8,16},{16,24},{24,32},{32,40},{40,48},{48,56},{56,0},{1,9},... | collective-permute-start | bytes 786440 | tf_op jit(solution)/shard_map/ppermute | solution.py:274
  35.0 10.8 %collective-permute-start.6 = (bf16[256,512]{1,0:T(8,128)(2,1)S(1)}, bf16[256,512]{1,0:T(8,128)(2,1)S(1)}, u32[]{:S(2)}, u32[]{:S(2)}) collective-permute-start(bf16[256,512]{1,0:T(8,128)(2,1)S(1)} %collective-permute-done.2.refs_2_), channel_id=1, source_target_pairs={{0,2},{2,0},{1,3},{3,1},{4,6},{6,4},{5,7},{7,5},{8,10},{10,8},{9,1... | collective-permute-start | bytes 786440 | tf_op jit(solution)/shard_map/ppermute | solution.py:275
  35.0 10.9 %collective-permute-start.8 = (bf16[256,512]{1,0:T(8,128)(2,1)S(1)}, bf16[256,512]{1,0:T(8,128)(2,1)}, u32[]{:S(2)}, u32[]{:S(2)}) collective-permute-start(bf16[256,512]{1,0:T(8,128)(2,1)S(1)} %collective-permute-done.2.refs_2_), channel_id=1, source_target_pairs={{0,56},{8,0},{16,8},{24,16},{32,24},{40,32},{48,40},{56,48},{1,57}... | collective-permute-start | bytes 786440 | tf_op jit(solution)/shard_map/ppermute | solution.py:274
  45.8 4.8 %copy-start.8 = (bf16[256,512]{1,0:T(8,128)(2,1)}, bf16[256,512]{1,0:T(8,128)(2,1)S(1)}, u32[]{:S(2)}) copy-start(bf16[256,512]{1,0:T(8,128)(2,1)S(1)} %collective-permute-done.5.refs_8_) | copy-start | bytes 786436
  45.8 4.8 %copy-start.10 = (bf16[256,512]{1,0:T(8,128)(2,1)}, bf16[256,512]{1,0:T(8,128)(2,1)S(1)}, u32[]{:S(2)}) copy-start(bf16[256,512]{1,0:T(8,128)(2,1)S(1)} %collective-permute-done.6.refs_9_) | copy-start | bytes 786436
  45.9 3.8 %collective-permute-start.9 = (bf16[512,512]{1,0:T(8,128)(2,1)S(1)}, bf16[512,512]{1,0:T(8,128)(2,1)S(1)}, u32[]{:S(2)}, u32[]{:S(2)}) collective-permute-start(bf16[512,512]{1,0:T(8,128)(2,1)S(1)} %get-tuple-element.44), channel_id=1, source_target_pairs={{0,2},{2,0},{1,3},{3,1},{4,6},{6,4},{5,7},{7,5},{8,10},{10,8},{9,1... | collective-permute-start | bytes 1572872 | tf_op jit(solution)/shard_map/ppermute | solution.py:305
  46.2 4.5 %collective-permute-start.10 = (bf16[256,512]{1,0:T(8,128)(2,1)}, bf16[256,512]{1,0:T(8,128)(2,1)S(1)}, u32[]{:S(2)}, u32[]{:S(2)}) collective-permute-start(bf16[256,512]{1,0:T(8,128)(2,1)} %collective-permute-done.7.refs_3_), channel_id=1, source_target_pairs={{0,2},{2,0},{1,3},{3,1},{4,6},{6,4},{5,7},{7,5},{8,10},{10,8},{9,1... | collective-permute-start | bytes 786440 | tf_op jit(solution)/shard_map/ppermute | solution.py:307
  46.5 11.6 %collective-permute-start.12 = (bf16[256,512]{1,0:T(8,128)(2,1)}, bf16[256,512]{1,0:T(8,128)(2,1)S(1)}, u32[]{:S(2)}, u32[]{:S(2)}) collective-permute-start(bf16[256,512]{1,0:T(8,128)(2,1)} %collective-permute-done.7.refs_3_), channel_id=1, source_target_pairs={{0,8},{8,16},{16,24},{24,32},{32,40},{40,48},{48,56},{56,0},{1,9},... | collective-permute-start | bytes 786440 | tf_op jit(solution)/shard_map/ppermute | solution.py:306
  46.5 4.2 %collective-permute-start.11 = (bf16[256,512]{1,0:T(8,128)(2,1)}, bf16[256,512]{1,0:T(8,128)(2,1)S(1)}, u32[]{:S(2)}, u32[]{:S(2)}) collective-permute-start(bf16[256,512]{1,0:T(8,128)(2,1)} %collective-permute-done.8.refs_4_), channel_id=1, source_target_pairs={{0,2},{2,0},{1,3},{3,1},{4,6},{6,4},{5,7},{7,5},{8,10},{10,8},{9,1... | collective-permute-start | bytes 786440 | tf_op jit(solution)/shard_map/ppermute | solution.py:307
  46.7 11.5 %collective-permute-start.13 = (bf16[256,512]{1,0:T(8,128)(2,1)}, bf16[256,512]{1,0:T(8,128)(2,1)S(1)}, u32[]{:S(2)}, u32[]{:S(2)}) collective-permute-start(bf16[256,512]{1,0:T(8,128)(2,1)} %collective-permute-done.8.refs_4_), channel_id=1, source_target_pairs={{0,56},{8,0},{16,8},{24,16},{32,24},{40,32},{48,40},{56,48},{1,57}... | collective-permute-start | bytes 786440 | tf_op jit(solution)/shard_map/ppermute | solution.py:306
  50.7 9.6 %copy-start.9 = (bf16[256,512]{1,0:T(8,128)(2,1)S(1)}, bf16[256,512]{1,0:T(8,128)(2,1)}, u32[]{:S(2)}) copy-start(bf16[256,512]{1,0:T(8,128)(2,1)} %copy-done.8) | copy-start | bytes 786436
  50.7 9.5 %copy-start.11 = (bf16[256,512]{1,0:T(8,128)(2,1)S(1)}, bf16[256,512]{1,0:T(8,128)(2,1)}, u32[]{:S(2)}) copy-start(bf16[256,512]{1,0:T(8,128)(2,1)} %copy-done.10) | copy-start | bytes 786436
  50.7 27.0 %all-to-all-start.2 = ((bf16[64,8,512]{2,1,0:T(8,128)(2,1)}), bf16[64,8,512]{2,1,0:T(8,128)(2,1)}, u32[]{:S(2)}, u32[]{:S(2)}) async-start(bf16[64,8,512]{2,1,0:T(8,128)(2,1)} %fusion), calls=%async_computation.2 | async-start | bytes 1048576 | tf_op jit(solution)/shard_map/all_to_all | solution.py:310
  58.0 2.3 %copy-start = (bf16[1,128,16,128]{3,2,1,0:T(8,128)(2,1)S(1)}, bf16[1,128,16,128]{3,2,1,0:T(8,128)(2,1)}, u32[]{:S(2)}) copy-start(bf16[1,128,16,128]{3,2,1,0:T(8,128)(2,1)} %param.8) | copy-start | bytes 1572868
  58.0 2.3 %copy-start.7 = (bf16[256,512]{1,0:T(8,128)(2,1)S(1)}, bf16[256,512]{1,0:T(8,128)(2,1)}, u32[]{:S(2)}) copy-start(bf16[256,512]{1,0:T(8,128)(2,1)} %copy-done.6) | copy-start | bytes 786436
  58.0 2.2 %collective-permute-start.15 = (bf16[256,512]{1,0:T(8,128)(2,1)S(1)}, bf16[256,512]{1,0:T(8,128)(2,1)S(1)}, u32[]{:S(2)}, u32[]{:S(2)}) collective-permute-start(bf16[256,512]{1,0:T(8,128)(2,1)S(1)} %collective-permute-done.12.first_ref.refs_5_), channel_id=1, source_target_pairs={{0,2},{2,0},{1,3},{3,1},{4,6},{6,4},{5,7},{7,5},{8,10},{10,8},{9,1... | collective-permute-start | bytes 786440 | tf_op jit(solution)/shard_map/ppermute | solution.py:345
  58.2 2.1 %collective-permute-start.16 = (bf16[256,512]{1,0:T(8,128)(2,1)S(1)}, bf16[256,512]{1,0:T(8,128)(2,1)S(1)}, u32[]{:S(2)}, u32[]{:S(2)}) collective-permute-start(bf16[256,512]{1,0:T(8,128)(2,1)S(1)} %collective-permute-done.13.second_ref.refs_6_), channel_id=1, source_target_pairs={{0,2},{2,0},{1,3},{3,1},{4,6},{6,4},{5,7},{7,5},{8,10},{10,8},{9,1... | collective-permute-start | bytes 786440 | tf_op jit(solution)/shard_map/ppermute | solution.py:345
  58.7 16.2 %collective-permute-start.14 = (bf16[256,512]{1,0:T(8,128)(2,1)S(1)}, bf16[256,512]{1,0:T(8,128)(2,1)S(1)}, u32[]{:S(2)}, u32[]{:S(2)}) collective-permute-start(bf16[256,512]{1,0:T(8,128)(2,1)S(1)} %pick.1), channel_id=1, source_target_pairs={{0,8},{2,58},{8,16},{10,2},{16,24},{18,10},{24,32},{26,18},{32,40}... | collective-permute-start | bytes 786440 | tf_op jit(solution)/shard_map/ppermute | solution.py:344
  74.8 1.5 %collective-permute-start.17 = (bf16[256,512]{1,0:T(8,128)(2,1)S(1)}, bf16[256,512]{1,0:T(8,128)(2,1)S(1)}, u32[]{:S(2)}, u32[]{:S(2)}) collective-permute-start(bf16[256,512]{1,0:T(8,128)(2,1)S(1)} %collective-permute-done.14.refs_0_), channel_id=1, source_target_pairs={{0,2},{2,0},{1,3},{3,1},{4,6},{6,4},{5,7},{7,5},{8,10},{10,8},{9,1... | collective-permute-start | bytes 786440 | tf_op jit(solution)/shard_map/ppermute | solution.py:360

commit v4 on v3

--- a/solution.py
+++ b/solution.py
@@ -124,8 +124,8 @@
 def blend(q_own, kv_ref, block, top_ref, sum_ref, acc_ref):
     for h in range(2):
         lane = h * 2 * HD
-        keys = kv_ref[block, :, lane : lane + HD]
-        values = with_ones(kv_ref[block, :, lane + HD : lane + 2 * HD])
+        keys = kv_ref[block, :, lane : lane + HD].reshape(-1, HD)
+        values = with_ones(kv_ref[block, :, lane + HD : lane + 2 * HD].reshape(-1, HD))
         for t in range(1024 // TILE):
             cols = slice(t * TILE, (t + 1) * TILE)
             state = top_ref[h, cols, :], sum_ref[h, cols, :], acc_ref[h, cols, :]
@@ -165,14 +165,21 @@
             state = attend(q_own[h, cols, :], keys, values, limit, start, zero, zero)
             top_ref[h, cols, :], sum_ref[h, cols, :], acc_ref[h, cols, :] = state
 
-    @pl.loop(1, NEAR)
-    def _(block):
-        wait_block(kv_ref, sems, block)
-        step = (block + 1) // 2
-
-        @pl.when(jnp.where(block % 2 == 1, z >= step, z + step >= 8))
+    @pl.loop(1, NEAR // 2 + 1)
+    def _(step):
+        first = 2 * step - 1
+        wait_block(kv_ref, sems, first)
+        wait_block(kv_ref, sems, first + 1)
+        up = z >= step
+        down = z + step >= 8
+
+        @pl.when(jnp.logical_and(up, down))
         def _():
-            blend(q_own, kv_ref, block, top_ref, sum_ref, acc_ref)
+            blend(q_own, kv_ref, pl.ds(first, 2), top_ref, sum_ref, acc_ref)
+
+        @pl.when(jnp.logical_xor(up, down))
+        def _():
+            blend(q_own, kv_ref, jnp.where(up, first, first + 1), top_ref, sum_ref, acc_ref)
 
     acc_out[...] = acc_ref[...] / sum_ref[...]
     lse_out[...] = top_ref[...] + jnp.log2(sum_ref[...])
@@ -337,9 +344,7 @@
         name="pick",
     )(up3, down3)
     halves = [
-        (zi * 2 + ci, (zi + (1 if ci == 0 else 7)) % 8 * 2 + ci)
-        for zi in range(8)
-        for ci in range(2)
+        ((zi + (1 if ci else 7)) % 8 * 2 + ci, zi * 2 + ci) for zi in range(4, 8) for ci in range(2)
     ]
     last = lax.ppermute(split, ("z", "c"), halves)
     up3c, down3c = lax.ppermute(up3, "c", swap), lax.ppermute(down3, "c", swap)

time: 80.9 us -> 78.9 us (0.975); the launches traced: 79.4 us -> 78.5 us
  waiting for transfers between devices: 17.3 us -> 8.24 us
  starting transfers between devices: 26.5 us -> 34.7 us
    ppermute x1, waiting for transfers between devices: 11.8 us -> 0.01 us  [shards(): last = lax.ppermute(split, ('z', 'c'), halves)]
    ppermute x1, starting transfers between devices: 0.01 us -> 9.12 us  [shards(): last_c = lax.ppermute(last, 'c', swap)]
    all_to_all x1, waiting for transfers between devices: 0.01 us -> 2.43 us  [shards(): pieces = lax.all_to_all(partial, ring, 0, 0, tiled=True)]
    ppermute x1, starting transfers between devices: 1.57 us -> 0.68 us  [shards(): last = lax.ppermute(split, ('z', 'c'), halves)]
  transfers between devices with their start and end apart: 20 -> 20, of which waited for: 4 -> 6; matrix products, arithmetic and copies ran while one was open for 1% -> 1% of each run, Pallas kernels for 16% -> 16%
where the time goes in v4:
time: 78.9 us; the launch traced here: 78.5 us
  starting transfers between devices  34.7 us (44%)
  blocking collectives  16.6 us (21%)
  Pallas kernels  14.5 us (18%)
  waiting for transfers between devices  8.24 us (10%)
  local copies, waits for them, and re-layouts  2.54 us (3%)
  other arithmetic  0.97 us (1%)
  between operations  0.87 us (1%)
    all_to_all x1, blocking collectives, shards(): column = lax.all_to_all(image, 'z', 0, 0, tiled=True).reshape(1, 64, 4 * HD)  16.6 us
    ppermute x1, starting transfers between devices, shards(): last_c = lax.ppermute(last, 'c', swap)  9.12 us
    pallas_call x1, Pallas kernels, shards(): pl.pallas_call(cross_kernel, grid=(2,), out_shape=(jax.ShapeDtypeStruct((...  8.15 us
    all_to_all x1, starting transfers between devices, shards(): pieces = lax.all_to_all(partial, ring, 0, 0, tiled=True)  7.28 us
    all_to_all x1, starting transfers between devices, shards(): lax.all_to_all(jnp.broadcast_to(column, (8, 64, 4 * HD)), ('y', 'x'), 0,...  4.87 us
    ppermute x2, waiting for transfers between devices, shards(): up1, down1 = (lax.ppermute(pair, 'z', up), lax.ppermute(pair, 'z', down))  3.69 us
    ppermute x2, starting transfers between devices, shards(): up1, down1 = (lax.ppermute(pair, 'z', up), lax.ppermute(pair, 'z', down))  3.31 us
    ppermute x2, starting transfers between devices, shards(): up2, down2 = (lax.ppermute(up1, 'z', up), lax.ppermute(down1, 'z', down))  3.24 us
  transfers between devices with their start and end apart: 20, of which 6 were waited for; matrix products, arithmetic and copies ran while one was open for 1% of the time, Pallas kernels for 16%

profile of v4, /device:TPU:4, one launch (start us, length us, event | category | flops | bytes accessed | tf_op | source)
XLA Modules:
  0.0 78.5 jit_solution(6413978678329511269)
XLA Ops:
  0.6 0.0 copy-start.12
  0.6 0.9 %copy.12 = bf16[16,8,2,256]{3,1,2,0:T(8,128)(2,1)S(1)} copy(bf16[16,8,2,256]{3,2,1,0:T(2,128)(2,1)} %bitcast.25) | data formatting | bytes 262144
  1.6 1.3 %collective-permute-start = (bf16[128,512]{1,0:T(8,128)(2,1)S(1)}, bf16[128,512]{1,0:T(8,128)(2,1)S(1)}, u32[]{:S(2)}, u32[]{:S(2)}) collective-permute-start(bf16[128,512]{1,0:T(8,128)(2,1)S(1)} %bitcast.19), channel_id=1, source_target_pairs={{0,4},{4,0},{1,5},{5,1},{2,6},{6,2},{3,7},{7,3},{8,12},{12,8},{9,1... | collective-permute-start | bytes 393224 | tf_op jit(solution)/shard_map/ppermute | solution.py:250
  2.9 0.0 copy-done.12
  2.9 16.6 %all_to_all.15 = bf16[8,8,512]{2,1,0:T(8,128)(2,1)S(1)} all-to-all(bf16[8,8,512]{2,1,0:T(8,128)(2,1)S(1)} %broadcast_in_dim.21), channel_id=1, replica_groups=mesh['y'=4,'z'=8,'x'=2,'c'=2,'t'=2] {'z'}, dimensions={0} | all-to-all | bytes 131072 | tf_op jit(solution)/shard_map/all_to_all | solution.py:251
  19.5 0.0 collective-permute-done.other_ref
  19.5 0.8 %broadcast_in_dim.23 = bf16[8,64,512]{2,1,0:T(8,128)(2,1)} broadcast(bf16[64,512]{1,0:T(8,128)(2,1)S(1)} %bitcast.24), dimensions={1,2} | broadcast | bytes 589824 | tf_op jit(solution)/shard_map/broadcast_in_dim | solution.py:262
  20.4 4.9 %all-to-all-start.1 = ((bf16[8,64,512]{2,1,0:T(8,128)(2,1)}), bf16[8,64,512]{2,1,0:T(8,128)(2,1)S(1)}, u32[]{:S(2)}, u32[]{:S(2)}) async-start(bf16[8,64,512]{2,1,0:T(8,128)(2,1)} %broadcast_in_dim.23), calls=%async_computation.1 | async-start | bytes 1048576 | tf_op jit(solution)/shard_map/all_to_all | solution.py:261
  25.2 0.0 copy-start.2
  25.2 0.0 copy-start.3
  25.2 0.0 copy-start.4
  25.3 0.6 collective-permute-start.1
  25.9 2.7 %collective-permute-start.2 = (bf16[256,512]{1,0:T(8,128)(2,1)S(1)}, bf16[256,512]{1,0:T(8,128)(2,1)S(1)}, u32[]{:S(2)}, u32[]{:S(2)}) collective-permute-start(bf16[256,512]{1,0:T(8,128)(2,1)S(1)} %pair.1.refs_0_), channel_id=1, source_target_pairs={{0,56},{8,0},{16,8},{24,16},{32,24},{40,32},{48,40},{56,48},{1,57}... | collective-permute-start | bytes 786440 | tf_op jit(solution)/shard_map/ppermute | solution.py:264
  28.6 0.0 collective-permute-start.3
  28.6 0.0 copy-done.1
  28.6 0.0 copy-done.2
  28.6 0.0 copy-done.3
  28.6 0.6 mask_and_gate.1
  29.3 3.7 %collective-permute-done.1.refs_1_ = bf16[256,512]{1,0:T(8,128)(2,1)S(1)} collective-permute-done((bf16[256,512]{1,0:T(8,128)(2,1)S(1)}, bf16[256,512]{1,0:T(8,128)(2,1)S(1)}, u32[]{:S(2)}, u32[]{:S(2)}) %collective-permute-start.1) | collective-permute-done | bytes 262176 | tf_op jit(solution)/shard_map/ppermute | solution.py:264
  33.0 0.0 collective-permute-done.2.refs_2_
  33.0 0.0 collective-permute-done.3.refs_7_
  33.0 0.7 copy-done.6
  33.7 0.2 all-to-all-done.1
  33.9 0.0 collective-permute-start.4
  33.9 0.5 collective-permute-start.5
  34.4 0.6 collective-permute-start.7
  35.0 0.0 collective-permute-start.6
  35.0 2.7 %collective-permute-start.8 = (bf16[256,512]{1,0:T(8,128)(2,1)S(1)}, bf16[256,512]{1,0:T(8,128)(2,1)}, u32[]{:S(2)}, u32[]{:S(2)}) collective-permute-start(bf16[256,512]{1,0:T(8,128)(2,1)S(1)} %collective-permute-done.2.refs_2_), channel_id=1, source_target_pairs={{0,56},{8,0},{16,8},{24,16},{32,24},{40,32},{48,40},{56,48},{1,57}... | collective-permute-start | bytes 786440 | tf_op jit(solution)/shard_map/ppermute | solution.py:281
  37.7 0.0 collective-permute-done.4.vb_ref
  37.7 0.0 copy-done.5
  37.7 8.2 %cross_attention.1 = (f32[128,16,128]{2,1,0:T(8,128)S(1)}, bf16[128,16,128]{2,1,0:T(8,128)(2,1)}, f32[512,512]{1,0:T(8,128)S(1)}, bf16[512,512]{1,0:T(8,128)(2,1)S(1)}) custom-call(f32[2,1024]{1,0:T(2,128)S(1)} %get-tuple-element.37.bias_ref, bf16[128,16,128]{2,1,0:T(8,128)(2,1)S(1)} %bitcast.21, bf16[128,16,128]{2,1,0:T(8,128)(2,1)S(1)} %bitcast.22, ...), custom_call_target="tpu_custom_call" | custom-call | flops 3221225472 | bytes 6291456 | tf_op jit(solution)/shard_map/cross_attention/pallas_call | solution.py:286
  45.8 0.0 collective-permute-done.5.refs_8_
  45.8 0.0 collective-permute-done.6.refs_9_
  45.8 0.0 collective-permute-done.7.refs_3_
  45.9 0.0 collective-permute-done.8.refs_4_
  45.9 0.3 collective-permute-start.9
  46.2 0.3 collective-permute-start.10
  46.5 0.0 collective-permute-start.12
  46.5 0.2 collective-permute-start.11
  46.7 3.0 %collective-permute-start.13 = (bf16[256,512]{1,0:T(8,128)(2,1)}, bf16[256,512]{1,0:T(8,128)(2,1)S(1)}, u32[]{:S(2)}, u32[]{:S(2)}) collective-permute-start(bf16[256,512]{1,0:T(8,128)(2,1)} %collective-permute-done.8.refs_4_), channel_id=1, source_target_pairs={{0,56},{8,0},{16,8},{24,16},{32,24},{40,32},{48,40},{56,48},{1,57}... | collective-permute-start | bytes 786440 | tf_op jit(solution)/shard_map/ppermute | solution.py:313
  49.7 0.0 collective-permute-done.9
  49.7 1.0 %fusion = bf16[64,8,512]{2,1,0:T(8,128)(2,1)} fusion(f32[512,512]{1,0:T(8,128)S(1)} %get-tuple-element.40, bf16[512,512]{1,0:T(8,128)(2,1)S(1)} %collective-permute-done.9), kind=kLoop, calls=%fused_computation.1 | loop fusion | flops 786432 | bytes 2097152 | tf_op jit(solution)/shard_map/reshape | solution.py:315
  50.7 0.0 copy-done.10
  50.7 0.0 collective-permute-done.10.refs_10_
  50.7 0.0 collective-permute-done.11.refs_11_
  50.7 0.0 copy-start.9
  50.7 7.3 %all-to-all-start.2 = ((bf16[64,8,512]{2,1,0:T(8,128)(2,1)}), bf16[64,8,512]{2,1,0:T(8,128)(2,1)}, u32[]{:S(2)}, u32[]{:S(2)}) async-start(bf16[64,8,512]{2,1,0:T(8,128)(2,1)} %fusion), calls=%async_computation.2 | async-start | bytes 1048576 | tf_op jit(solution)/shard_map/all_to_all | solution.py:317
  58.0 0.0 copy-start
  58.0 0.0 collective-permute-done.12.first_ref.refs_5_
  58.0 0.1 collective-permute-start.15
  58.1 0.0 collective-permute-done.13.second_ref.refs_6_
  58.2 0.5 collective-permute-start.16
  58.7 0.7 collective-permute-start.14
  59.4 0.3 collective-permute-done.15.refs_12_
  59.7 0.4 collective-permute-done.16.refs_13_
  60.0 0.0 copy-done
  60.0 0.0 copy-done.7
  60.1 2.7 %self_near.1 = (f32[2,1024,128]{2,1,0:T(8,128)S(1)}, f32[2,1024,128]{2,1,0:T(8,128)S(1)}) custom-call(bf16[256,512]{1,0:T(8,128)(2,1)S(1)} %pair.1.refs_0_, bf16[256,512]{1,0:T(8,128)(2,1)S(1)} %collective-permute-done.1.refs_1_, bf16[256,512]{1,0:T(8,128)(2,1)S(1)} %collective-permute-done.2.refs_2_, bf16[256,512]{1,0:T(8,128)(2,1)} %collective-permute-done.7.refs_3_, ...), custom_call_target="tpu_custom_call" | custom-call | flops 3758096384 | bytes 6291456 | tf_op jit(solution)/shard_map/self_near/pallas_call | solution.py:353
  62.7 0.0 collective-permute-done.14.refs_0_
  62.8 9.1 %collective-permute-start.17 = (bf16[256,512]{1,0:T(8,128)(2,1)S(1)}, bf16[256,512]{1,0:T(8,128)(2,1)S(1)}, u32[]{:S(2)}, u32[]{:S(2)}) collective-permute-start(bf16[256,512]{1,0:T(8,128)(2,1)S(1)} %collective-permute-done.14.refs_0_), channel_id=1, source_target_pairs={{0,2},{2,0},{1,3},{3,1},{4,6},{6,4},{5,7},{7,5},{8,10},{10,8},{9,1... | collective-permute-start | bytes 786440 | tf_op jit(solution)/shard_map/ppermute | solution.py:365
  71.9 1.2 %collective-permute-done.17.refs_1_ = bf16[256,512]{1,0:T(8,128)(2,1)S(1)} collective-permute-done((bf16[256,512]{1,0:T(8,128)(2,1)S(1)}, bf16[256,512]{1,0:T(8,128)(2,1)S(1)}, u32[]{:S(2)}, u32[]{:S(2)}) %collective-permute-start.17) | collective-permute-done | bytes 262176 | tf_op jit(solution)/shard_map/ppermute | solution.py:365
  73.0 1.3 %self_far.1 = bf16[128,16,128]{2,1,0:T(8,128)(2,1)} custom-call(bf16[256,512]{1,0:T(8,128)(2,1)S(1)} %collective-permute-done.14.refs_0_, bf16[256,512]{1,0:T(8,128)(2,1)S(1)} %collective-permute-done.17.refs_1_, bf16[128,16,128]{2,1,0:T(8,128)(2,1)S(1)} %bitcast.16, f32[2,1024,128]{2,1,0:T(8,128)S(1)} %get-tuple-element.55.refs_3_, ...), custom_call_target="tpu_custom_call" | custom-call | flops 536870912 | bytes 6291456 | tf_op jit(solution)/shard_map/self_far/pallas_call | solution.py:366
  74.3 2.4 %all-to-all-done.2.pieces_ref = bf16[64,8,512]{2,1,0:T(8,128)(2,1)} async-done(((bf16[64,8,512]{2,1,0:T(8,128)(2,1)}), bf16[64,8,512]{2,1,0:T(8,128)(2,1)}, u32[]{:S(2)}, u32[]{:S(2)}) %all-to-all-start.2) | async-done | bytes 524320 | tf_op jit(solution)/shard_map/all_to_all | solution.py:317
  76.8 1.7 %sum_pieces.1 = f32[8,2,256]{2,1,0:T(2,128)} custom-call(bf16[64,8,512]{2,1,0:T(8,128)(2,1)} %all-to-all-done.2.pieces_ref), custom_call_target="tpu_custom_call" | custom-call | tf_op jit(solution)/shard_map/sum_pieces/pallas_call | solution.py:378
  (15 shorter events, 0.1 us)
Async XLA Ops:
  0.6 2.2 %copy-start.12 = (bf16[8,2,256]{2,1,0:T(2,128)(2,1)S(1)}, bf16[8,2,256]{2,1,0:T(2,128)(2,1)}, u32[]{:S(2)}) copy-start(bf16[8,2,256]{2,1,0:T(2,128)(2,1)} %param.11) | copy-start | bytes 24580
  1.6 17.9 %collective-permute-start = (bf16[128,512]{1,0:T(8,128)(2,1)S(1)}, bf16[128,512]{1,0:T(8,128)(2,1)S(1)}, u32[]{:S(2)}, u32[]{:S(2)}) collective-permute-start(bf16[128,512]{1,0:T(8,128)(2,1)S(1)} %bitcast.19), channel_id=1, source_target_pairs={{0,4},{4,0},{1,5},{5,1},{2,6},{6,2},{3,7},{7,3},{8,12},{12,8},{9,1... | collective-permute-start | bytes 393224 | tf_op jit(solution)/shard_map/ppermute | solution.py:250
  20.4 17.3 %copy-start.5 = (bf16[1,128,16,128]{3,2,1,0:T(8,128)(2,1)S(1)}, bf16[1,128,16,128]{3,2,1,0:T(8,128)(2,1)}, u32[]{:S(2)}) copy-start(bf16[1,128,16,128]{3,2,1,0:T(8,128)(2,1)} %param.15) | copy-start | bytes 1572868
  20.4 13.6 %all-to-all-start.1 = ((bf16[8,64,512]{2,1,0:T(8,128)(2,1)}), bf16[8,64,512]{2,1,0:T(8,128)(2,1)S(1)}, u32[]{:S(2)}, u32[]{:S(2)}) async-start(bf16[8,64,512]{2,1,0:T(8,128)(2,1)} %broadcast_in_dim.23), calls=%async_computation.1 | async-start | bytes 1048576 | tf_op jit(solution)/shard_map/all_to_all | solution.py:261
  25.2 3.4 %copy-start.1 = (s32[2,4]{1,0:T(2,128)S(1)}, s32[2,4]{1,0:T(2,128)}, u32[]{:S(2)}) copy-start(s32[2,4]{1,0:T(2,128)} %mask_ref.1) | copy-start | bytes 100
  25.2 3.4 %copy-start.2 = (s32[4]{0:T(128)S(1)}, s32[4]{0:T(128)}, u32[]{:S(2)}) copy-start(s32[4]{0:T(128)} %image_ref.1) | copy-start | bytes 52
  25.2 3.4 %copy-start.3 = (f32[1,16]{1,0:T(1,128)S(1)}, f32[1,16]{1,0:T(1,128)}, u32[]{:S(2)}) copy-start(f32[1,16]{1,0:T(1,128)} %gate_ref.1) | copy-start | bytes 196
  25.2 12.4 %copy-start.4 = (bf16[1,128,16,128]{3,2,1,0:T(8,128)(2,1)S(1)}, bf16[1,128,16,128]{3,2,1,0:T(8,128)(2,1)}, u32[]{:S(2)}) copy-start(bf16[1,128,16,128]{3,2,1,0:T(8,128)(2,1)} %param.10) | copy-start | bytes 1572868
  25.3 7.7 %collective-permute-start.1 = (bf16[256,512]{1,0:T(8,128)(2,1)S(1)}, bf16[256,512]{1,0:T(8,128)(2,1)S(1)}, u32[]{:S(2)}, u32[]{:S(2)}) collective-permute-start(bf16[256,512]{1,0:T(8,128)(2,1)S(1)} %pair.1.refs_0_), channel_id=1, source_target_pairs={{0,8},{8,16},{16,24},{24,32},{32,40},{40,48},{48,56},{56,0},{1,9},... | collective-permute-start | bytes 786440 | tf_op jit(solution)/shard_map/ppermute | solution.py:264
  25.9 7.0 %collective-permute-start.2 = (bf16[256,512]{1,0:T(8,128)(2,1)S(1)}, bf16[256,512]{1,0:T(8,128)(2,1)S(1)}, u32[]{:S(2)}, u32[]{:S(2)}) collective-permute-start(bf16[256,512]{1,0:T(8,128)(2,1)S(1)} %pair.1.refs_0_), channel_id=1, source_target_pairs={{0,56},{8,0},{16,8},{24,16},{32,24},{40,32},{48,40},{56,48},{1,57}... | collective-permute-start | bytes 786440 | tf_op jit(solution)/shard_map/ppermute | solution.py:264
  28.6 4.4 %collective-permute-start.3 = (bf16[256,512]{1,0:T(8,128)(2,1)S(1)}, bf16[256,512]{1,0:T(8,128)(2,1)S(1)}, u32[]{:S(2)}, u32[]{:S(2)}) collective-permute-start(bf16[256,512]{1,0:T(8,128)(2,1)S(1)} %pair.1.refs_0_), channel_id=1, source_target_pairs={{0,2},{2,0},{1,3},{3,1},{4,6},{6,4},{5,7},{7,5},{8,10},{10,8},{9,1... | collective-permute-start | bytes 786440 | tf_op jit(solution)/shard_map/ppermute | solution.py:265
  33.0 0.7 copy-start.6
  33.9 3.8 %collective-permute-start.4 = (bf16[512,512]{1,0:T(8,128)(2,1)S(1)}, bf16[512,512]{1,0:T(8,128)(2,1)S(1)}, u32[]{:S(2)}, u32[]{:S(2)}) collective-permute-start(bf16[512,512]{1,0:T(8,128)(2,1)S(1)} %bitcast.17), channel_id=1, source_target_pairs={{0,2},{2,0},{1,3},{3,1},{4,6},{6,4},{5,7},{7,5},{8,10},{10,8},{9,1... | collective-permute-start | bytes 1572872 | tf_op jit(solution)/shard_map/ppermute | solution.py:280
  33.9 11.9 %collective-permute-start.5 = (bf16[256,512]{1,0:T(8,128)(2,1)S(1)}, bf16[256,512]{1,0:T(8,128)(2,1)S(1)}, u32[]{:S(2)}, u32[]{:S(2)}) collective-permute-start(bf16[256,512]{1,0:T(8,128)(2,1)S(1)} %collective-permute-done.1.refs_1_), channel_id=1, source_target_pairs={{0,2},{2,0},{1,3},{3,1},{4,6},{6,4},{5,7},{7,5},{8,10},{10,8},{9,1... | collective-permute-start | bytes 786440 | tf_op jit(solution)/shard_map/ppermute | solution.py:282
  34.4 11.4 %collective-permute-start.7 = (bf16[256,512]{1,0:T(8,128)(2,1)S(1)}, bf16[256,512]{1,0:T(8,128)(2,1)}, u32[]{:S(2)}, u32[]{:S(2)}) collective-permute-start(bf16[256,512]{1,0:T(8,128)(2,1)S(1)} %collective-permute-done.1.refs_1_), channel_id=1, source_target_pairs={{0,8},{8,16},{16,24},{24,32},{32,40},{40,48},{48,56},{56,0},{1,9},... | collective-permute-start | bytes 786440 | tf_op jit(solution)/shard_map/ppermute | solution.py:281
  35.0 10.8 %collective-permute-start.6 = (bf16[256,512]{1,0:T(8,128)(2,1)S(1)}, bf16[256,512]{1,0:T(8,128)(2,1)S(1)}, u32[]{:S(2)}, u32[]{:S(2)}) collective-permute-start(bf16[256,512]{1,0:T(8,128)(2,1)S(1)} %collective-permute-done.2.refs_2_), channel_id=1, source_target_pairs={{0,2},{2,0},{1,3},{3,1},{4,6},{6,4},{5,7},{7,5},{8,10},{10,8},{9,1... | collective-permute-start | bytes 786440 | tf_op jit(solution)/shard_map/ppermute | solution.py:282
  35.0 10.9 %collective-permute-start.8 = (bf16[256,512]{1,0:T(8,128)(2,1)S(1)}, bf16[256,512]{1,0:T(8,128)(2,1)}, u32[]{:S(2)}, u32[]{:S(2)}) collective-permute-start(bf16[256,512]{1,0:T(8,128)(2,1)S(1)} %collective-permute-done.2.refs_2_), channel_id=1, source_target_pairs={{0,56},{8,0},{16,8},{24,16},{32,24},{40,32},{48,40},{56,48},{1,57}... | collective-permute-start | bytes 786440 | tf_op jit(solution)/shard_map/ppermute | solution.py:281
  45.8 4.8 %copy-start.8 = (bf16[256,512]{1,0:T(8,128)(2,1)}, bf16[256,512]{1,0:T(8,128)(2,1)S(1)}, u32[]{:S(2)}) copy-start(bf16[256,512]{1,0:T(8,128)(2,1)S(1)} %collective-permute-done.5.refs_8_) | copy-start | bytes 786436
  45.8 4.8 %copy-start.10 = (bf16[256,512]{1,0:T(8,128)(2,1)}, bf16[256,512]{1,0:T(8,128)(2,1)S(1)}, u32[]{:S(2)}) copy-start(bf16[256,512]{1,0:T(8,128)(2,1)S(1)} %collective-permute-done.6.refs_9_) | copy-start | bytes 786436
  45.9 3.8 %collective-permute-start.9 = (bf16[512,512]{1,0:T(8,128)(2,1)S(1)}, bf16[512,512]{1,0:T(8,128)(2,1)S(1)}, u32[]{:S(2)}, u32[]{:S(2)}) collective-permute-start(bf16[512,512]{1,0:T(8,128)(2,1)S(1)} %get-tuple-element.44), channel_id=1, source_target_pairs={{0,2},{2,0},{1,3},{3,1},{4,6},{6,4},{5,7},{7,5},{8,10},{10,8},{9,1... | collective-permute-start | bytes 1572872 | tf_op jit(solution)/shard_map/ppermute | solution.py:312
  46.2 4.5 %collective-permute-start.10 = (bf16[256,512]{1,0:T(8,128)(2,1)}, bf16[256,512]{1,0:T(8,128)(2,1)S(1)}, u32[]{:S(2)}, u32[]{:S(2)}) collective-permute-start(bf16[256,512]{1,0:T(8,128)(2,1)} %collective-permute-done.7.refs_3_), channel_id=1, source_target_pairs={{0,2},{2,0},{1,3},{3,1},{4,6},{6,4},{5,7},{7,5},{8,10},{10,8},{9,1... | collective-permute-start | bytes 786440 | tf_op jit(solution)/shard_map/ppermute | solution.py:314
  46.5 11.6 %collective-permute-start.12 = (bf16[256,512]{1,0:T(8,128)(2,1)}, bf16[256,512]{1,0:T(8,128)(2,1)S(1)}, u32[]{:S(2)}, u32[]{:S(2)}) collective-permute-start(bf16[256,512]{1,0:T(8,128)(2,1)} %collective-permute-done.7.refs_3_), channel_id=1, source_target_pairs={{0,8},{8,16},{16,24},{24,32},{32,40},{40,48},{48,56},{56,0},{1,9},... | collective-permute-start | bytes 786440 | tf_op jit(solution)/shard_map/ppermute | solution.py:313
  46.5 4.2 %collective-permute-start.11 = (bf16[256,512]{1,0:T(8,128)(2,1)}, bf16[256,512]{1,0:T(8,128)(2,1)S(1)}, u32[]{:S(2)}, u32[]{:S(2)}) collective-permute-start(bf16[256,512]{1,0:T(8,128)(2,1)} %collective-permute-done.8.refs_4_), channel_id=1, source_target_pairs={{0,2},{2,0},{1,3},{3,1},{4,6},{6,4},{5,7},{7,5},{8,10},{10,8},{9,1... | collective-permute-start | bytes 786440 | tf_op jit(solution)/shard_map/ppermute | solution.py:314
  46.7 11.5 %collective-permute-start.13 = (bf16[256,512]{1,0:T(8,128)(2,1)}, bf16[256,512]{1,0:T(8,128)(2,1)S(1)}, u32[]{:S(2)}, u32[]{:S(2)}) collective-permute-start(bf16[256,512]{1,0:T(8,128)(2,1)} %collective-permute-done.8.refs_4_), channel_id=1, source_target_pairs={{0,56},{8,0},{16,8},{24,16},{32,24},{40,32},{48,40},{56,48},{1,57}... | collective-permute-start | bytes 786440 | tf_op jit(solution)/shard_map/ppermute | solution.py:313
  50.7 9.3 %copy-start.9 = (bf16[256,512]{1,0:T(8,128)(2,1)S(1)}, bf16[256,512]{1,0:T(8,128)(2,1)}, u32[]{:S(2)}) copy-start(bf16[256,512]{1,0:T(8,128)(2,1)} %copy-done.8) | copy-start | bytes 786436
  50.7 9.3 %copy-start.11 = (bf16[256,512]{1,0:T(8,128)(2,1)S(1)}, bf16[256,512]{1,0:T(8,128)(2,1)}, u32[]{:S(2)}) copy-start(bf16[256,512]{1,0:T(8,128)(2,1)} %copy-done.10) | copy-start | bytes 786436
  50.7 26.1 %all-to-all-start.2 = ((bf16[64,8,512]{2,1,0:T(8,128)(2,1)}), bf16[64,8,512]{2,1,0:T(8,128)(2,1)}, u32[]{:S(2)}, u32[]{:S(2)}) async-start(bf16[64,8,512]{2,1,0:T(8,128)(2,1)} %fusion), calls=%async_computation.2 | async-start | bytes 1048576 | tf_op jit(solution)/shard_map/all_to_all | solution.py:317
  58.0 2.0 %copy-start = (bf16[1,128,16,128]{3,2,1,0:T(8,128)(2,1)S(1)}, bf16[1,128,16,128]{3,2,1,0:T(8,128)(2,1)}, u32[]{:S(2)}) copy-start(bf16[1,128,16,128]{3,2,1,0:T(8,128)(2,1)} %param.8) | copy-start | bytes 1572868
  58.0 2.0 %copy-start.7 = (bf16[256,512]{1,0:T(8,128)(2,1)S(1)}, bf16[256,512]{1,0:T(8,128)(2,1)}, u32[]{:S(2)}) copy-start(bf16[256,512]{1,0:T(8,128)(2,1)} %copy-done.6) | copy-start | bytes 786436
  58.0 1.6 %collective-permute-start.15 = (bf16[256,512]{1,0:T(8,128)(2,1)S(1)}, bf16[256,512]{1,0:T(8,128)(2,1)S(1)}, u32[]{:S(2)}, u32[]{:S(2)}) collective-permute-start(bf16[256,512]{1,0:T(8,128)(2,1)S(1)} %collective-permute-done.12.first_ref.refs_5_), channel_id=1, source_target_pairs={{0,2},{2,0},{1,3},{3,1},{4,6},{6,4},{5,7},{7,5},{8,10},{10,8},{9,1... | collective-permute-start | bytes 786440 | tf_op jit(solution)/shard_map/ppermute | solution.py:350
  58.2 1.9 %collective-permute-start.16 = (bf16[256,512]{1,0:T(8,128)(2,1)S(1)}, bf16[256,512]{1,0:T(8,128)(2,1)S(1)}, u32[]{:S(2)}, u32[]{:S(2)}) collective-permute-start(bf16[256,512]{1,0:T(8,128)(2,1)S(1)} %collective-permute-done.13.second_ref.refs_6_), channel_id=1, source_target_pairs={{0,2},{2,0},{1,3},{3,1},{4,6},{6,4},{5,7},{7,5},{8,10},{10,8},{9,1... | collective-permute-start | bytes 786440 | tf_op jit(solution)/shard_map/ppermute | solution.py:350
  58.7 4.1 %collective-permute-start.14 = (bf16[256,512]{1,0:T(8,128)(2,1)S(1)}, bf16[256,512]{1,0:T(8,128)(2,1)S(1)}, u32[]{:S(2)}, u32[]{:S(2)}) collective-permute-start(bf16[256,512]{1,0:T(8,128)(2,1)S(1)} %pick.1), channel_id=1, source_target_pairs={{24,32},{42,34},{32,40},{50,42},{40,48},{58,50},{48,56},{2,58},{25... | collective-permute-start | bytes 786440 | tf_op jit(solution)/shard_map/ppermute | solution.py:349
  62.8 10.3 %collective-permute-start.17 = (bf16[256,512]{1,0:T(8,128)(2,1)S(1)}, bf16[256,512]{1,0:T(8,128)(2,1)S(1)}, u32[]{:S(2)}, u32[]{:S(2)}) collective-permute-start(bf16[256,512]{1,0:T(8,128)(2,1)S(1)} %collective-permute-done.14.refs_0_), channel_id=1, source_target_pairs={{0,2},{2,0},{1,3},{3,1},{4,6},{6,4},{5,7},{7,5},{8,10},{10,8},{9,1... | collective-permute-start | bytes 786440 | tf_op jit(solution)/shard_map/ppermute | solution.py:365
